TPU v7x, 32 devices: a whole 2x2x4 slice. The times are simulated.
32 devices in a mesh: dp: 8 (over y, x, core), seq: 4 (over z).
Axes of the slice: x: 2, y: 2, z: 4, core: 2. Of those that a mesh axis runs over, the one named last changes fastest.
Arguments:
- hidden_in: bfloat16 [8, 1024, 2048], P('dp', 'seq'), may hold values from -6 to 6
- q_weight: bfloat16 [2048, 2048], P(('dp', 'seq')), may hold values from -0.125 to 0.125
- k_weight: bfloat16 [2048, 2048], P(('dp', 'seq')), may hold values from -0.125 to 0.125
- v_weight: bfloat16 [2048, 2048], P(('dp', 'seq')), may hold values from -0.125 to 0.125
- o_weight: bfloat16 [2048, 2048], P(('dp', 'seq')), may hold values from -0.125 to 0.125
- q_gain: bfloat16 [2048], P(('dp', 'seq')), may hold values from 0.099609375 to 1.8984375
- k_gain: bfloat16 [2048], P(('dp', 'seq')), may hold values from 0.099609375 to 1.8984375
- attn_gain: bfloat16 [2048], P(('dp', 'seq')), may hold values from 0.099609375 to 1.8984375
- gate_weight: bfloat16 [2048, 8192], P(('dp', 'seq')), may hold values from -0.125 to 0.125
- up_weight: bfloat16 [2048, 8192], P(('dp', 'seq')), may hold values from -0.125 to 0.125
- down_weight: bfloat16 [8192, 2048], P(('dp', 'seq')), may hold values from -0.0625 to 0.0625
- mlp_gain: bfloat16 [2048], P(('dp', 'seq')), may hold values from 0.099609375 to 1.8984375
- out_grad: bfloat16 [8, 1024, 2048], P('dp', 'seq'), may hold values from -6 to 6
Outputs:
- layer_out: bfloat16 [8, 1024, 2048], P('dp', 'seq')
- in_grad: bfloat16 [8, 1024, 2048], P('dp', 'seq')
- q_weight_grad: float32 [2048, 2048], P(('dp', 'seq'))
- k_weight_grad: float32 [2048, 2048], P(('dp', 'seq'))
- v_weight_grad: float32 [2048, 2048], P(('dp', 'seq'))
- o_weight_grad: float32 [2048, 2048], P(('dp', 'seq'))
- gate_weight_grad: float32 [2048, 8192], P(('dp', 'seq'))
- up_weight_grad: float32 [2048, 8192], P(('dp', 'seq'))
- down_weight_grad: float32 [8192, 2048], P(('dp', 'seq'))
- q_gain_grad: float32 [2048], P(('dp', 'seq'))
- k_gain_grad: float32 [2048], P(('dp', 'seq'))
- attn_gain_grad: float32 [2048], P(('dp', 'seq'))
- mlp_gain_grad: float32 [2048], P(('dp', 'seq'))
All inputs are finite; a program needn't handle non-finite values.
Results may differ from a plain program's by a relative error of at most 0.02.
Values may be sent and summed in bfloat16 or wider, within the bound.
No kernel may reach another device: no remote copies, remote signals or barrier semaphores. Data moves between devices by JAX's collectives and lax.ppermute only.
A program may use at most 512 MiB of HBM per device.

v0:
```python
import math

import jax
import jax.numpy as jnp
from jax import lax
from jax.experimental import pallas as pl
from jax.experimental.pallas import tpu as pltpu
from jax.sharding import Mesh
from jax.sharding import PartitionSpec as P

HEADS = 16
EPSILON = 1e-06
ROPE_THETA = 500000.0
LOW = jnp.bfloat16
FULL = jnp.float32

AXES = ("g", "e", "x", "c", "h", "l")
SWAP = [(0, 1), (1, 0)]
BOTH = [(i, 3 - i) for i in range(4)]
VMEM_LIMIT = 56 * 1024 * 1024


BLOCK = 256

def dot_nt(a, b):
    return lax.dot_general(a, b, (((1,), (1,)), ((), ())), preferred_element_type=FULL)

def dot_nn(a, b):
    return lax.dot_general(a, b, (((1,), (0,)), ((), ())), preferred_element_type=FULL)

def dot_tn(a, b):
    return lax.dot_general(a, b, (((0,), (0,)), ((), ())), preferred_element_type=FULL)

def turn(tensor):
    return pltpu.roll(tensor, tensor.shape[1] // 2, 1)


def attend_kernel(q_raw, k_raw, v_raw, inverse, q_gain, k_gain, cosine, sine,
                  q_out, k_out, v_out, mixed):
    length, head_dim = q_raw.shape
    factor = 1.0 / math.sqrt(head_dim)
    block = min(BLOCK, length)

    def rope(raw, column, gain):
        normed = raw[...] * inverse[:, column : column + 1] * gain[...]
        return (normed * cosine[...] + turn(normed) * sine[...]).astype(LOW)

    q_out[...] = rope(q_raw, 0, q_gain)
    k_out[...] = rope(k_raw, 1, k_gain)
    v_out[...] = v_raw[...].astype(LOW)
    shape = (block, block)
    allowed = lax.broadcasted_iota(jnp.int32, shape, 1) <= lax.broadcasted_iota(jnp.int32, shape, 0)
    for start in range(0, length, block):
        here = slice(start, start + block)
        queries = q_out[here, :]
        near = jnp.where(allowed, dot_nt(queries, k_out[here, :]) * factor, -1e30)
        top = jnp.max(near, axis=1, keepdims=True)
        if start:
            far = dot_nt(queries, k_out[:start, :]) * factor
            top = jnp.maximum(top, jnp.max(far, axis=1, keepdims=True))
            far = jnp.exp(far - top)
        near = jnp.exp(near - top)
        total = jnp.sum(near, axis=1, keepdims=True)
        if start:
            total += jnp.sum(far, axis=1, keepdims=True)
        scale = 1.0 / total
        out = dot_nn((near * scale).astype(LOW), v_out[here, :])
        if start:
            out += dot_nn((far * scale).astype(LOW), v_out[:start, :])
        mixed[here, :] = out.astype(LOW)


def attend(raw, inverse, q_gain, k_gain, cosine, sine):
    length = raw.shape[0]
    head_dim = cosine.shape[1]
    width = q_gain.shape[1]
    heads = width // head_dim
    column = lambda shift: pl.BlockSpec((length, head_dim), lambda i: (0, i + shift * heads))
    whole = lambda v: pl.BlockSpec(v.shape, lambda i: (0, 0))
    gain = pl.BlockSpec((1, head_dim), lambda i: (0, i))
    out = jax.ShapeDtypeStruct((length, width), LOW)
    return pl.pallas_call(
        attend_kernel,
        grid=(heads,),
        in_specs=[column(0), column(1), column(2), whole(inverse), gain, gain, whole(cosine), whole(sine)],
        out_specs=[column(0)] * 4,
        out_shape=[out] * 4,
        compiler_params=pltpu.CompilerParams(vmem_limit_bytes=VMEM_LIMIT),
        cost_estimate=pl.CostEstimate(flops=0, bytes_accessed=0, transcendentals=0),
    )(raw, raw, raw, inverse, q_gain, k_gain, cosine, sine)


def attend_back_kernel(queries, keys, values, mixed_grad, q_raw, k_raw, inverse, q_gain, k_gain, cosine, sine,
                       q_grad, k_grad, v_grad, sums, q_gain_grad, k_gain_grad, k_total, v_total):
    length, head_dim = queries.shape
    factor = 1.0 / math.sqrt(head_dim)
    block = min(BLOCK, length)
    shape = (block, block)
    allowed = lax.broadcasted_iota(jnp.int32, shape, 0) <= lax.broadcasted_iota(jnp.int32, shape, 1)
    first = pl.program_id(0) == 0

    def unrope(grad, raw, column, gain, rows):
        pre = grad * cosine[rows, :] - turn(grad) * sine[rows, :]
        unit = raw[rows, :] * inverse[rows, column : column + 1]
        scaled = pre * gain[...]
        return scaled, jnp.sum(scaled * unit, axis=1, keepdims=True), jnp.sum(pre * unit, axis=0, keepdims=True)

    q_gain_total = jnp.zeros((1, head_dim), FULL)
    for start in range(0, length, block):
        here = slice(start, start + block)
        query, out_grad = queries[here, :], mixed_grad[here, :]
        near = jnp.where(allowed, dot_nt(keys[here, :], query) * factor, -1e30)
        top = jnp.max(near, axis=0, keepdims=True)
        if start:
            far = dot_nt(keys[:start, :], query) * factor
            top = jnp.maximum(top, jnp.max(far, axis=0, keepdims=True))
            far = jnp.exp(far - top)
        near = jnp.exp(near - top)
        total = jnp.sum(near, axis=0, keepdims=True)
        if start:
            total += jnp.sum(far, axis=0, keepdims=True)
        scale = 1.0 / total
        near = near * scale
        near_grad = dot_nt(values[here, :], out_grad)
        inner = jnp.sum(near * near_grad, axis=0, keepdims=True)
        if start:
            far = far * scale
            far_grad = dot_nt(values[:start, :], out_grad)
            inner += jnp.sum(far * far_grad, axis=0, keepdims=True)
        near_score = (near * (near_grad - inner) * factor).astype(LOW)
        grad = dot_tn(near_score, keys[here, :])
        k_total[here, :] = dot_nn(near_score, query)
        v_total[here, :] = dot_nn(near.astype(LOW), out_grad)
        if start:
            far_score = (far * (far_grad - inner) * factor).astype(LOW)
            grad += dot_tn(far_score, keys[:start, :])
            k_total[:start, :] += dot_nn(far_score, query)
            v_total[:start, :] += dot_nn(far.astype(LOW), out_grad)
        scaled, row_sum, gain_part = unrope(grad, q_raw, 0, q_gain, here)
        q_grad[here, :] = scaled
        q_gain_total += gain_part
        sums[here, 0:1] = jnp.where(first, row_sum, sums[here, 0:1] + row_sum)
    q_gain_grad[...] = q_gain_total
    scaled, row_sum, gain_part = unrope(k_total[...], k_raw, 1, k_gain, slice(None))
    k_grad[...] = scaled
    k_gain_grad[...] = gain_part
    sums[:, 1:2] = jnp.where(first, row_sum, sums[:, 1:2] + row_sum)
    v_grad[...] = v_total[...].astype(LOW)


def attend_back(
    queries, keys, values, mixed_grad, raw, inverse, q_gain, k_gain, cosine, sine, waits
):
    length, width = queries.shape
    head_dim = cosine.shape[1]
    heads = width // head_dim
    column = lambda shift: pl.BlockSpec((length, head_dim), lambda i: (0, i + shift * heads))
    whole = lambda v: pl.BlockSpec(v.shape, lambda i: (0, 0))
    gain = pl.BlockSpec((1, head_dim), lambda i: (0, i))
    wide = jax.ShapeDtypeStruct((length, width), FULL)
    vector = jax.ShapeDtypeStruct((1, width), FULL)
    def body(*refs):
        attend_back_kernel(*refs[:11], *refs[11 + len(waits) :])

    return pl.pallas_call(
        body,
        grid=(heads,),
        in_specs=[column(0)] * 4 + [column(0), column(1), whole(inverse), gain, gain, whole(cosine), whole(sine)]
        + [pl.BlockSpec(memory_space=pl.ANY)] * len(waits),
        out_specs=[column(0)] * 3 + [pl.BlockSpec((length, 2), lambda i: (0, 0)), gain, gain],
        out_shape=[wide, wide, jax.ShapeDtypeStruct((length, width), LOW), jax.ShapeDtypeStruct((length, 2), FULL), vector, vector],
        scratch_shapes=[pltpu.VMEM((length, head_dim), FULL)] * 2,
        compiler_params=pltpu.CompilerParams(vmem_limit_bytes=VMEM_LIMIT),
        cost_estimate=pl.CostEstimate(flops=0, bytes_accessed=0, transcendentals=0),
    )(queries, keys, values, mixed_grad, raw, raw, inverse, q_gain, k_gain, cosine, sine, *waits)

def call(kernel, grid, inputs, outputs, waits=(), scalars=(), work=2**33):
    count = len(scalars) + len(inputs)

    def body(*refs):
        kernel(*refs[:count], *refs[count + len(waits) :])

    out = pl.pallas_call(
        body,
        grid=grid,
        in_specs=[spec for _, spec in scalars]
        + [pl.BlockSpec(block, index) for _, block, index in inputs]
        + [pl.BlockSpec(memory_space=pl.ANY)] * len(waits),
        out_specs=[pl.BlockSpec(block, index) for _, _, block, index in outputs],
        out_shape=[jax.ShapeDtypeStruct(shape, kind) for shape, kind, _, _ in outputs],
        compiler_params=pltpu.CompilerParams(vmem_limit_bytes=VMEM_LIMIT),
        cost_estimate=pl.CostEstimate(flops=work, bytes_accessed=0, transcendentals=0),
    )(*(v for v, _ in scalars), *(v for v, _, _ in inputs), *waits)
    return out[0] if len(outputs) == 1 else out


def stay(array):
    return array, array.shape, lambda *i: (0,) * array.ndim


def chip_product(places, lefts, weights, product, width, tile):
    length = lefts[0][0].shape[-2]
    count = length // 16
    inputs = lefts + weights

    def rows_of(ref, chip):
        parts = []
        for z in range(4):
            start = pl.multiple_of((z * 4 + chip) * count, count)
            parts.append(ref[pl.ds(start, count), :])
        return jnp.concatenate(parts, axis=0)

    def part(place, refs, flip_e, flip_x):
        e = 1 - place[0] if flip_e else place[0]
        x = 1 - place[1] if flip_x else place[1]
        rows = [rows_of(ref, e * 2 + x) for ref in refs[: len(lefts)]]
        out = product(rows, *refs[len(lefts) : len(inputs)])
        return out.astype(LOW).reshape(4, count, tile)

    def kernel(place, *refs):
        far = part(place, refs, True, True)
        refs[-5][...] = far[:2]
        refs[-4][...] = far[2:]
        refs[-3][...] = part(place, refs, True, False)
        refs[-2][...] = part(place, refs, False, True)
        refs[-1][...] = part(place, refs, False, False)

    out = lambda parts: (
        (parts, count, width), LOW, (parts, count, tile), lambda j: (0, 0, j),
    )
    outs = [out(2), out(2), out(4), out(4), out(4)]
    smem = pl.BlockSpec(memory_space=pltpu.SMEM)
    return call(kernel, (width // tile,), inputs, outs, (), [(places, smem)])


ATTN_TILE = 512


def feature_blocks(groups, rows):
    size = 8 * rows
    for g in range(groups):
        for k in range(4):
            start = (g * 4 + k) * size
            yield slice(start, start + size), slice(g * 8, g * 8 + 8), k


def project(all_in, weights):
    length = all_in.shape[0]
    eight, four, rows, _ = weights.shape
    tile = ATTN_TILE

    def kernel(a, w, out):
        total = jnp.zeros(out.shape, FULL)
        for columns, pieces, k in feature_blocks(eight // 8, rows):
            total += dot_nn(a[:, columns], w[pieces, k].reshape(8 * rows, tile))
        out[...] = total

    return call(
        kernel,
        (3,),
        [stay(all_in), (weights, (eight, four, rows, tile), lambda j: (0, 0, 0, j + 1))],
        [((length, 3 * tile), FULL, (length, tile), lambda j: (0, j))],
    )


def project_back(places, raw_grad, weights):
    eight, four, rows, columns = weights.shape
    tile = ATTN_TILE
    size = 8 * rows

    def product(lefts, w):
        return dot_nt(lefts[0], w[:, 0, :, tile : 4 * tile].reshape(size, 3 * tile))

    weight = (weights, (8, 1, rows, columns), lambda j: (j // 4, j % 4, 0, 0))
    width = eight // 8 * 4 * size
    return chip_product(places, [stay(raw_grad)], [weight], product, width, size)


def mix_out(places, mixed, weights):
    eight, four, rows, _ = weights.shape
    features = mixed.shape[1]
    tile = ATTN_TILE

    def product(lefts, w):
        return dot_nn(lefts[0], w[:, 0].reshape(features, tile))

    weight = (weights, (eight, 1, rows, tile), lambda j: (0, j, 0, 0))
    return chip_product(places, [stay(mixed)], [weight], product, four * tile, tile)


def mix_out_back(attn_grad, weights):
    length, width = attn_grad.shape
    eight, four, rows, _ = weights.shape
    tile = ATTN_TILE
    features = eight * rows
    part = min(length, 256)

    def kernel(a, w, out):
        total = jnp.zeros(out.shape, FULL)
        for k in range(four):
            right = w[:, k].reshape(features, tile)
            total += dot_nt(a[:, k * tile : (k + 1) * tile], right)
        out[...] = total.astype(LOW)

    return call(
        kernel,
        (length // part,),
        [
            (attn_grad, (part, width), lambda j: (j, 0)),
            (weights, (eight, four, rows, tile), lambda j: (0, 0, 0, 0)),
        ],
        [((length, features), LOW, (part, features), lambda j: (j, 0))],
    )


def gated(mlp_in, weights, waits):
    length = mlp_in.shape[0]
    eight, _, four, rows, count = weights.shape
    tile = min(count, 512)

    def kernel(a, gate_w, up_w, hidden, gate, up):
        both = []
        for w in (gate_w, up_w):
            total = jnp.zeros(gate.shape, FULL)
            for columns, pieces, k in feature_blocks(eight // 8, rows):
                total += dot_nn(a[:, columns], w[pieces, 0, k].reshape(8 * rows, tile))
            both.append(total)
        gate[...], up[...] = both
        hidden[...] = (both[0] * jax.nn.sigmoid(both[0]) * both[1]).astype(LOW)

    weight = lambda i: (
        weights, (eight, 1, four, rows, tile), lambda j: (0, i, 0, 0, j),
    )
    cut = ((length, tile), lambda j: (0, j))
    shape = (length, count)
    return call(
        kernel,
        (count // tile,),
        [stay(mlp_in), weight(0), weight(1)],
        [(shape, LOW) + cut, (shape, FULL) + cut, (shape, FULL) + cut],
        waits,
    )


def branch_out(places, hidden, weights):
    units = hidden.shape[1]
    eight, _, four, rows, width = weights.shape
    tile = min(width, 512)

    def product(lefts, w):
        return dot_nn(lefts[0], w[:, 0].reshape(units, tile))

    weight = (weights, (eight, 1, four, rows, tile), lambda j: (0, 2, 0, 0, j))
    return chip_product(places, [stay(hidden)], [weight], product, width, tile)


def gated_back(branch_rows, weights, gate_raw, up_raw):
    length, units = gate_raw.shape
    eight, _, four, rows, width = weights.shape
    tile = min(units, 512)
    pieces = tile // (four * rows)

    def kernel(a, w, gate, up, out):
        hidden_grad = dot_nt(a[...], w[:, 0].reshape(tile, width))
        raw = gate[...]
        sigmoid = jax.nn.sigmoid(raw)
        slope = sigmoid * (1.0 + raw * (1.0 - sigmoid))
        out[0] = (hidden_grad * up[...] * slope).astype(LOW)
        out[1] = (hidden_grad * raw * sigmoid).astype(LOW)

    cut = ((length, tile), lambda j: (0, j))
    return call(
        kernel,
        (units // tile,),
        [
            stay(branch_rows),
            (weights, (pieces, 1, four, rows, width), lambda j: (j, 2, 0, 0, 0)),
            (gate_raw,) + cut,
            (up_raw,) + cut,
        ],
        [((2, length, units), LOW, (2, length, tile), lambda j: (0, 0, j))],
    )


def input_back(places, grads, weights):
    _, length, units = grads.shape
    eight, _, four, rows, _ = weights.shape
    size = 8 * rows

    def product(lefts, gate_w, up_w):
        gate = dot_nt(lefts[0], gate_w[:, 0, 0].reshape(size, units))
        return gate + dot_nt(lefts[1], up_w[:, 0, 0].reshape(size, units))

    left = lambda i: (grads, (None, length, units), lambda j: (i, 0, 0))
    weight = lambda i: (
        weights, (8, 1, 1, rows, units), lambda j: (j // 4, i, j % 4, 0, 0),
    )
    width = eight // 8 * four * size
    return chip_product(
        places, [left(0), left(1)], [weight(0), weight(1)], product, width, size
    )


def down_grad(hidden, branch_rows, groups, rows):
    length, units = hidden[0].shape
    width = branch_rows[0].shape[1]
    run = 4 * rows
    many = 1 if run % 128 == 0 else 4
    shape = (4, groups, run, width)

    def kernel(a, b, c, d, out):
        total = dot_tn(a[...], b[...]) + dot_tn(c[...], d[...])
        out[...] = total.astype(LOW).reshape(out.shape)

    cut = ((length, many * run), lambda g, j: (0, g * (4 // many) + j))
    return call(
        kernel,
        (groups, 4 // many),
        [
            (hidden[0],) + cut,
            stay(branch_rows[0]),
            (hidden[1],) + cut,
            stay(branch_rows[1]),
        ],
        [(shape, LOW, (many, 1, run, width), lambda g, j: (j, g, 0, 0))],
    )


def lay_features(total, out, many, rows):
    for i in range(many):
        for j in range(4):
            start = (i * 4 + j) * rows
            yield (j, i), total[start : start + rows]


def units_grad(mlp_in, grads, groups, rows):
    length = mlp_in[0].shape[0]
    units = grads[0].shape[2]
    run = 4 * rows
    many = 1 if run % 128 == 0 else 4
    shape = (4, 2, groups, 4, rows, units)

    def kernel(a, b, c, d, out):
        total = (dot_tn(a[...], b[0]) + dot_tn(c[...], d[0])).astype(LOW)
        for (j, i), part in lay_features(total, out, many, rows):
            out[j, 0, 0, i] = part

    cut = ((length, many * run), lambda i, g, j: (0, g * (4 // many) + j))
    right = ((1, length, units), lambda i, g, j: (i, 0, 0))
    return call(
        kernel,
        (2, groups, 4 // many),
        [
            (mlp_in[0],) + cut,
            (grads[0],) + right,
            (mlp_in[1],) + cut,
            (grads[1],) + right,
        ],
        [
            (
                shape,
                LOW,
                (4, 1, 1, many, rows, units),
                lambda i, g, j: (0, i, g, j, 0, 0),
            )
        ],
    )


def attention_grad(all_in, raw_grad, mixed, attn_grad, groups, rows, waits):
    length = all_in[0].shape[0]
    tile = ATTN_TILE
    run = 4 * rows
    many = 1 if run % 128 == 0 else 4
    shape = (4, groups, 4, rows, 4 * tile)

    def kernel(a, b, c, d, e, f, p, q, out):
        total = (dot_tn(a[...], b[...]) + dot_tn(c[...], d[...])).astype(LOW)
        for (j, i), part in lay_features(total, out, many, rows):
            out[j, 0, i, :, tile:] = part
        total = (dot_tn(e[0], f[...]) + dot_tn(p[0], q[...])).astype(LOW)
        for i in range(many):
            for j in range(4):
                part = total[j * rows : (j + 1) * rows, i * tile : (i + 1) * tile]
                out[j, 0, i, :, :tile] = part

    cut = ((length, many * run), lambda g, j: (0, g * (4 // many) + j))
    left = ((1, length, run), lambda g, j: (g, 0, 0))
    right = ((length, many * tile), lambda g, j: (0, j))
    return call(
        kernel,
        (groups, 4 // many),
        [
            (all_in[0],) + cut,
            stay(raw_grad[0]),
            (all_in[1],) + cut,
            stay(raw_grad[1]),
            (mixed[0],) + left,
            (attn_grad[0],) + right,
            (mixed[1],) + left,
            (attn_grad[1],) + right,
        ],
        [(shape, LOW, (4, 1, many, rows, 4 * tile), lambda g, j: (0, g, j, 0, 0))],
        waits,
    )


def wide(value):
    return value.astype(FULL)


def tie(values, others):
    if not others:
        return tuple(values)
    return lax.optimization_barrier(tuple(values) + tuple(others))[: len(values)]


def two_halves(first, second, waits):
    half = (first.shape[0] // 2,) + first.shape[1:]

    def kernel(a, b, a_out, b_out):
        a_out[...] = a[...]
        b_out[...] = b[...]

    out = (half, first.dtype, half, lambda i: (0, 0, 0))
    return call(
        kernel,
        (1,),
        [(first, half, lambda i: (0, 0, 0)), (second, half, lambda i: (1, 0, 0))],
        [out, out],
        waits,
        work=0,
    )


def hold(value, *others):
    def kernel(a, out):
        out[...] = a[...]

    shape = value.shape
    whole = (shape, lambda i: (0,) * len(shape))
    return call(kernel, (1,), [(value,) + whole], [(shape, value.dtype) + whole], others, work=0)


class Steps:
    def __init__(self):
        self.last = ()

    def wait(self, *values):
        self.last += tuple(jax.tree.leaves(values))

    def __call__(self, step, *inputs):
        flat, tree = jax.tree.flatten(inputs)
        out = step(*tree.unflatten(tie(flat, self.last)))
        self.last = tuple(jax.tree.leaves(out))
        return out


class Links:
    def __init__(self, steps):
        self.steps = steps

    def send(self, value, axes, pairs):
        (value,) = tie((value,), self.steps.last)
        return lax.ppermute(value, axes, pairs)

    def swap(self, value, axis):
        return self.send(value, axis, SWAP)

    def swap_both(self, value, first, second):
        return self.send(value, (first, second), BOTH)


def swap(value, axis):
    return lax.ppermute(value, axis, SWAP)


def pick(value, places):
    starts = [0] * value.ndim
    sizes = list(value.shape)
    for dim, place in places.items():
        starts[dim] = place
        sizes[dim] = 1
    taken = lax.dynamic_slice(value, starts, sizes)
    return taken.reshape([s for d, s in enumerate(value.shape) if d not in places])


def put(out, parts):
    for value, starts in parts:
        out = lax.dynamic_update_slice(out, value, starts)
    return out


class Place:
    def __init__(self):
        self.g, self.e, self.x, self.c, self.h, self.l = (lax.axis_index(a) for a in AXES)
        self.groups = lax.axis_size("g")
        self.steps = Steps()
        self.links = Links(self.steps)


class Spread:
    def __init__(self, at, part, inputs, first="e", second="x"):
        self.at, self.places = at, (getattr(at, first), getattr(at, second))
        a, b = self.places

        def start(*inputs):
            return tuple(part(i, j, *inputs) for i in (a, 1 - a) for j in (b, 1 - b))

        self.mine, for_b, for_a, far = at.steps(start, *inputs)
        self.from_a = at.links.swap(for_a, first)
        self.from_b = at.links.swap(for_b, second)
        self.far = at.links.swap_both(far, first, second)
        self.sent = (self.mine, for_b, for_a, far)
        self.came = (self.from_a, self.from_b, self.far)

    def second(self, lay):
        a, b = self.places

        def join(mine, from_a, from_b, far):
            return lay(
                [(mine, a, b), (from_a, 1 - a, b), (from_b, a, 1 - b), (far, 1 - a, 1 - b)]
            )

        return self.at.steps(join, self.mine, self.from_a, self.from_b, self.far)


def one_of(i, j, parts):
    return pick(parts, {0: i, 1: j})


def lay_all(parts):
    shape = parts[0][0].shape
    out = jnp.zeros((2, 2) + shape, parts[0][0].dtype)
    tail = (0,) * len(shape)
    return put(out, [(v.reshape((1, 1) + shape), (i, j) + tail) for v, i, j in parts])


class TokensIn:
    def __init__(self, at, rows):
        self.at = at
        self.spread = Spread(at, one_of, [rows.reshape(2, 2, -1, rows.shape[1])])

    def second(self):
        self.spread = Spread(self.at, one_of, [self.spread.second(lay_all)], "h", "l")

    def third(self):
        def lay(parts):
            out = lay_all(parts)
            return out.reshape((4,) + out.shape[2:])

        return self.spread.second(lay)


class TokensOut:
    def __init__(self, at, blocks):
        self.at = at
        blocks = blocks.reshape((2, 2) + blocks.shape[1:])
        self.spread = Spread(at, one_of, [blocks], "h", "l")

    def second(self):
        self.spread = Spread(self.at, one_of, [self.spread.second(lay_all)])

    def third(self):
        def lay(parts):
            out = lay_all(parts)
            return out.reshape(-1, out.shape[-1])

        return self.spread.second(lay)


class GatherTokens:
    def __init__(self, at, blocks):
        self.at, self.blocks = at, blocks
        self.from_e = at.links.swap(blocks, "e")
        self.from_x = at.links.swap(blocks, "x")

    def second(self, waits=()):
        at = self.at
        half_e, half_x = at.steps(two_halves, self.from_e, self.from_x, waits)
        self.far_0 = at.links.swap(half_e, "x")
        self.far_1 = at.links.swap(half_x, "e")
        four, count, width = self.blocks.shape
        cut = (four, 1, 1, count, width)

        def near(blocks, from_x, from_e):
            out = jnp.zeros((four, 2, 2, count, width), blocks.dtype)
            parts = [
                (blocks.reshape(cut), (0, at.e, at.x, 0, 0)),
                (from_x.reshape(cut), (0, at.e, 1 - at.x, 0, 0)),
                (from_e.reshape(cut), (0, 1 - at.e, at.x, 0, 0)),
            ]
            return put(out, parts)

        self.out = at.steps(near, self.blocks, self.from_x, self.from_e)

    def third(self):
        at = self.at
        four, count, width = self.blocks.shape
        cut = (2, 1, 1, count, width)

        def far(out, far_0, far_1):
            parts = [
                (far_0.reshape(cut), (0, 1 - at.e, 1 - at.x, 0, 0)),
                (far_1.reshape(cut), (2, 1 - at.e, 1 - at.x, 0, 0)),
            ]
            return put(out, parts).reshape(-1, width)

        return at.steps(far, self.out, self.far_0, self.far_1)


class ScatterTokens:
    def __init__(self, at, product, *inputs):
        self.at = at
        far_0, far_1, self.for_e, self.for_x, self.mine = at.steps(product, *inputs)
        self.for_e_0 = at.links.swap(far_0, "x")
        self.for_x_1 = at.links.swap(far_1, "e")

    def second(self):
        at = self.at

        def add(for_e, for_x, for_e_0, for_x_1):
            for_e_0 = (wide(for_e[:2]) + wide(for_e_0)).astype(LOW)
            for_x_1 = (wide(for_x[2:]) + wide(for_x_1)).astype(LOW)
            return jnp.concatenate([for_e_0, for_e[2:]]), jnp.concatenate([for_x[:2], for_x_1])

        for_e, for_x = at.steps(add, self.for_e, self.for_x, self.for_e_0, self.for_x_1)
        self.from_e = at.links.swap(for_e, "e")
        self.from_x = at.links.swap(for_x, "x")

    def third(self, step, *inputs):
        def add(mine, from_e, from_x, *inputs):
            return step(wide(mine) + wide(from_e) + wide(from_x), *inputs)

        return self.at.steps(add, self.mine, self.from_e, self.from_x, *inputs)


def sum_chips(value):
    far = lax.ppermute(value, ("e", "x"), BOTH)
    return value + swap(value, "x") + swap(value, "e") + far


def gather(at, piece, *others):
    (piece,) = tie((piece,), at.steps.last + others)
    return lax.all_gather(piece, ("g", "c", "h", "l"), axis=0)


def scatter(at, value, *others):
    (value,) = tie((value,), at.steps.last + others)
    value = lax.psum_scatter(value, ("h", "l"), scatter_dimension=0)
    return value


def scatter_groups(at, value, dim):
    if at.groups == 1:
        return value.reshape([n for d, n in enumerate(value.shape) if d != dim])
    return lax.psum_scatter(value, "g", scatter_dimension=dim)


def halves(value, core, runs):
    rows, count = value.shape
    each = count // (2 * runs)

    def of(place):
        parts = [
            lax.dynamic_slice(value, (0, (2 * k + place) * each), (rows, each))
            for k in range(runs)
        ]
        return jnp.concatenate(parts, axis=1)

    return of(core), of(1 - core)


class ScatterGains:
    def __init__(self, at, grads):
        self.at = at
        value = grads.reshape(grads.shape[0], at.groups, 2, 2, 2, 2, 2, -1)
        if at.groups > 1:
            value = lax.psum_scatter(value, "g", scatter_dimension=1, tiled=True)
        self.value = value.reshape(value.shape[:1] + value.shape[2:])
        self.axes = ["e", "x", "c", "h", "l"]
        self.start()

    def start(self):
        place = getattr(self.at, self.axes[0])
        self.kept, send = self.at.steps(
            lambda v: (pick(v, {1: place}), pick(v, {1: 1 - place})), self.value
        )
        self.got = self.at.links.swap(send, self.axes.pop(0))

    def more(self, waits=()):
        self.value = self.at.steps(lambda a, b: a + b, self.kept, self.got)
        if waits:
            self.value = hold(self.value, *waits)
        if self.axes:
            self.start()
        return self.value


def rope_tables(places, head_dim):
    half_dim = head_dim // 2
    inverse = jnp.power(
        jnp.float32(ROPE_THETA), -(jnp.arange(half_dim, dtype=FULL) * 2.0 / head_dim)
    )
    angles = places.astype(FULL)[:, None] * inverse[None, :]
    sine = jnp.sin(angles)
    cosine = jnp.cos(angles)
    return (
        jnp.concatenate([cosine, cosine], axis=-1),
        jnp.concatenate([-sine, sine], axis=-1),
    )


def norm_forward(tensor, gain_vec):
    inverse = lax.rsqrt(jnp.mean(tensor * tensor, axis=-1, keepdims=True) + EPSILON)
    unit = tensor * inverse
    return unit * gain_vec, unit, inverse


def norm_backward(grad_in, unit, inverse, gain_vec):
    axes = tuple(range(grad_in.ndim - 1))
    gain_grad = jnp.sum(grad_in * unit, axis=axes)
    unit_grad = grad_in * gain_vec
    inner = jnp.mean(unit_grad * unit, axis=-1, keepdims=True)
    return inverse * (unit_grad - unit * inner), gain_grad


def on_device(
    hidden_in,
    q_weight,
    k_weight,
    v_weight,
    o_weight,
    q_gain,
    k_gain,
    attn_gain,
    gate_weight,
    up_weight,
    down_weight,
    mlp_gain,
    out_grad,
):
    at = Place()
    steps = at.steps
    batch, rows_here, width = hidden_in.shape
    head_dim = width // HEADS
    length = batch * rows_here * 4
    rows_owned = q_weight.shape[0]
    groups = at.groups
    ff_block = down_weight.shape[0]

    assert head_dim % (8 * rows_owned) == 0 or (8 * rows_owned) % head_dim == 0
    assert ff_block == 4 * rows_owned

    def columns_of(e, x, weight):
        rows, count = weight.shape
        part = count // (4 * groups)
        each = [
            lax.dynamic_slice(weight, (0, ((g * 2 + e) * 2 + x) * part), (rows, part))
            for g in range(groups)
        ]
        return jnp.concatenate(each, axis=1)

    def lay_columns(parts):
        rows, count = parts[0][0].shape
        part = count // groups
        out = jnp.zeros((rows, 4 * count), FULL)
        for value, e, x in parts:
            for g in range(groups):
                piece = wide(value[:, g * part : (g + 1) * part])
                out = lax.dynamic_update_slice(out, piece, (0, ((g * 2 + e) * 2 + x) * part))
        return out

    quarter = width // 4

    def columns_of_attention(e, x, q, k, v, o, gains):
        three = [columns_of(e, x, w) for w in (q, k, v)]
        return jnp.concatenate(three + [gains], axis=1)

    def lay_attention(parts):
        tail = lay_all(parts)
        tail = tail.reshape((4,) + tail.shape[2:])
        runs = jnp.stack([o_weight[:, k * quarter : (k + 1) * quarter] for k in range(4)])
        return jnp.concatenate([runs, tail], axis=2)

    def lay_four(parts):
        out = lay_all(parts)
        return out.reshape((4,) + out.shape[2:])

    def lay_three(parts):
        return tuple(
            lay_columns([(v[:, i * quarter : (i + 1) * quarter], e, x) for v, e, x in parts])
            for i in range(3)
        )

    places = jnp.stack([at.e, at.x]).astype(jnp.int32)

    def here(vector):
        return pick(vector.reshape(groups, 2, 2, -1), {1: at.e, 2: at.x}).reshape(1, -1)

    def whole(vector):
        out = jnp.zeros((groups, 2, 2, vector.size // groups), FULL)
        part = vector.reshape(groups, 1, 1, -1)
        return lax.dynamic_update_slice(out, part, (0, at.e, at.x, 0)).reshape(-1)

    def pair(halved, core_sent):
        return halved, at.links.swap(core_sent, "c")

    gains = jnp.stack([q_gain, k_gain, attn_gain, mlp_gain], axis=1)
    gains = jnp.pad(gains, ((0, 0), (0, 124)))
    attn_spread = Spread(
        at, columns_of_attention, [q_weight, k_weight, v_weight, o_weight, gains]
    )
    own = TokensIn(at, hidden_in.reshape(-1, width))
    gate_spread = Spread(at, columns_of, [gate_weight])
    up_spread = Spread(at, columns_of, [up_weight])
    attn_all = gather(at, attn_spread.second(lay_attention))
    own.second()
    cosine, sine = steps(lambda n: rope_tables(n, head_dim), jnp.arange(length))
    gate_mine = gate_spread.second(lay_four)
    up_mine = up_spread.second(lay_four)
    mlp_mine = steps(
        lambda *v: jnp.stack(v), gate_mine, up_mine, down_weight.reshape((4, -1, width))
    )
    mlp_all = gather(at, mlp_mine)
    own_in = own.third()
    all_in = GatherTokens(at, own_in)
    all_in.second()
    all_in = all_in.third()
    all_in_half = pair(*steps(lambda v: halves(v, at.c, 4 * groups), all_in))
    top = TokensIn(at, out_grad.reshape(-1, width))
    steps.wait(all_in_half)

    def gains_of(weights):
        value = wide(weights[..., -128:-124]).reshape(groups, 8, 4, rows_owned, 4)
        return value.transpose(4, 0, 2, 1, 3).reshape(4, -1)

    gains = steps(gains_of, attn_all)
    q_gain_here, k_gain_here = here(gains[0]), here(gains[1])
    attn_gain_all, mlp_gain_all = gains[2], gains[3]

    def squares_of(raw):
        q_raw, k_raw = jnp.split(raw[:, : 2 * quarter], 2, axis=1)
        return jnp.stack([jnp.sum(q_raw * q_raw, -1), jnp.sum(k_raw * k_raw, -1)])

    raw = steps(project, all_in, attn_all)
    squares = sum_chips(steps(squares_of, raw))
    inverse = steps(lambda s: lax.rsqrt(s / width + EPSILON).T, squares)
    queries, keys, values, mixed = steps(
        attend, raw, inverse, q_gain_here, k_gain_here, cosine, sine
    )
    attn_out = ScatterTokens(at, mix_out, places, mixed, attn_all)

    def halve_mixed(mixed):
        return [
            v.reshape(length, groups, -1).swapaxes(0, 1) for v in halves(mixed, at.c, groups)
        ]

    mixed_half = pair(*steps(halve_mixed, mixed))
    steps.wait(mixed_half)
    attn_out.second()

    def after_attention(attn_out, own_in, gain):
        normed, unit, inverse = norm_forward(attn_out, gain)
        residual = wide(own_in) + normed
        return residual.astype(LOW), residual, unit, inverse

    residual_low, residual, attn_unit, attn_inverse = attn_out.third(
        after_attention, own_in, attn_gain_all
    )

    mlp_in = GatherTokens(at, residual_low)
    mlp_in.second()
    mlp_in = mlp_in.third()
    mlp_in_half = pair(*steps(lambda v: halves(v, at.c, 4 * groups), mlp_in))
    steps.wait(mlp_in_half)
    hidden, gate_raw, up_raw = steps(gated, mlp_in, mlp_all, top.spread.came)
    top.second()
    branch = ScatterTokens(at, branch_out, places, hidden, mlp_all)
    hidden_half = pair(*steps(lambda v: halves(v, at.c, groups), hidden))
    steps.wait(hidden_half)
    branch.second()
    own_top = top.third()

    def after_mlp(branch, residual, own_top, gain):
        normed, unit, inverse = norm_forward(branch, gain)
        grad, gain_grad = norm_backward(wide(own_top), unit, inverse, gain)
        return grad.astype(LOW), (residual + normed).astype(LOW), gain_grad

    branch_low, own_out, mlp_gain_grad = branch.third(
        after_mlp, residual, own_top, mlp_gain_all
    )

    branch_rows = GatherTokens(at, branch_low)
    layer_out = TokensOut(at, own_out)
    branch_rows.second(layer_out.spread.came)
    branch_rows = branch_rows.third()
    branch_rows = (branch_rows, at.links.swap(branch_rows, "c"))
    unit_grads = steps(gated_back, branch_rows[0], mlp_all, gate_raw, up_raw)
    unit_grads = (unit_grads, at.links.swap(unit_grads, "c"))
    grad = steps(lambda a, b: down_grad(a, b, groups, rows_owned), hidden_half, branch_rows)
    down_own = scatter(at, grad)
    input_part = ScatterTokens(at, input_back, places, unit_grads[0], mlp_all)
    grad = steps(lambda a, b: units_grad(a, b, groups, rows_owned), mlp_in_half, unit_grads)
    units_own = scatter(at, grad)
    input_part.second()
    layer_out.second()
    layer_out_came = layer_out.spread.came

    def before_attention(input_grad, own_top, unit, inverse, gain):
        residual_grad = wide(own_top) + input_grad
        grad, gain_grad = norm_backward(residual_grad, unit, inverse, gain)
        return grad.astype(LOW), residual_grad, gain_grad

    attn_grad, residual_grad, attn_gain_grad = input_part.third(
        before_attention, own_top, attn_unit, attn_inverse, attn_gain_all
    )

    attn_low = GatherTokens(at, attn_grad)
    layer_out = layer_out.third()
    attn_low.second()
    attn_low = attn_low.third()
    attn_low = (attn_low, swap(attn_low, "c"))
    mixed_grad = steps(mix_out_back, attn_low[0], attn_all)
    q_scaled, k_scaled, v_low, inner, q_gain_grad, k_gain_grad = steps(
        attend_back, queries, keys, values, mixed_grad, raw, inverse,
        q_gain_here, k_gain_here, cosine, sine, (down_own,) + layer_out_came,
    )
    inner = sum_chips(steps(lambda v: v.T / width, inner))

    def before_project(raw, inverse, q_scaled, k_scaled, v_low, inner):
        q_raw, k_raw = jnp.split(raw[:, : 2 * quarter], 2, axis=1)
        inner = inner.T
        grads = []
        for i, (part, scaled) in enumerate([(q_raw, q_scaled), (k_raw, k_scaled)]):
            each = inverse[:, i : i + 1]
            grads.append((each * (scaled - part * each * inner[:, i : i + 1])).astype(LOW))
        return jnp.concatenate(grads + [v_low], axis=1)

    raw_grad = steps(before_project, raw, inverse, q_scaled, k_scaled, v_low, inner)
    raw_grad = (raw_grad, swap(raw_grad, "c"))
    in_part = ScatterTokens(at, project_back, places, raw_grad[0], attn_all)
    attn_grad_part = steps(
        lambda *v: attention_grad(*v[:-1], groups, rows_owned, v[-1:]),
        all_in_half, raw_grad, mixed_half, attn_low, units_own,
    )
    attn_own = scatter(at, attn_grad_part)
    in_part.second()
    gains = jnp.stack([whole(q_gain_grad), whole(k_gain_grad), attn_gain_grad, mlp_gain_grad])
    gains = ScatterGains(at, gains)
    in_grad = in_part.third(lambda a, b: (a + b).astype(LOW), residual_grad)
    in_grad = TokensOut(at, in_grad)
    gains.more()
    gains.more()
    units_own = scatter_groups(at, units_own, 1)
    gate_spread = Spread(at, one_of, [units_own[0].reshape(2, 2, rows_owned, -1)])
    up_spread = Spread(at, one_of, [units_own[1].reshape(2, 2, rows_owned, -1)])
    gate_own = gate_spread.second(lay_columns)
    up_own = up_spread.second(lay_columns)
    in_grad.second()
    attn_own = scatter_groups(at, attn_own, 0)
    attn_spread = Spread(
        at, one_of, [attn_own[..., quarter:].reshape(2, 2, rows_owned, -1)]
    )
    gains.more(attn_spread.sent)
    in_grad = in_grad.third()
    o_own = wide(jnp.concatenate([attn_own[k, :, :quarter] for k in range(4)], axis=1))
    gains.more()
    own_three = list(attn_spread.second(lay_three))
    down_own = wide(scatter_groups(at, down_own, 0))
    gains = gains.more()
    shape = hidden_in.shape
    grads = own_three + [o_own, gate_own, up_own, down_own]
    return (layer_out.reshape(shape), in_grad.reshape(shape)) + tuple(grads) + tuple(gains)


def solution(mesh):
    dp, seq = mesh.shape["dp"], mesh.shape["seq"]
    split = Mesh(mesh.devices.reshape(dp // 8, 2, 2, 2, seq // 2, 2), AXES)
    dp_axes, seq_axes = AXES[:4], AXES[4:]
    tokens = P(dp_axes, seq_axes, None)
    matrix, vector = P(AXES, None), P(AXES)
    return jax.shard_map(
        on_device,
        mesh=split,
        in_specs=(tokens,)
        + (matrix,) * 4
        + (vector,) * 3
        + (matrix,) * 3
        + (vector, tokens),
        out_specs=(tokens,) * 2 + (matrix,) * 7 + (vector,) * 4,
        check_vma=False,
    )
```

profile of v0, /device:TPU:0, one launch (start us, length us, event | category | flops | bytes accessed | tf_op | source)
XLA Modules:
  0.0 907.4 jit_solution(12608037147864856825)
XLA Ops:
  12.1 3.9 collective-permute-start.5
  18.6 3.8 collective-permute-done.5
  22.4 4.0 collective-permute-done.4
  37.2 3.8 collective-permute-done.2
  43.3 3.3 collective-permute-done.1
  54.9 8.6 collective-permute-done.11
  64.8 3.2 collective-permute-done.10
  74.1 3.6 collective-permute-start.8
  78.6 12.2 %collective-permute-done.8 = bf16[64,2048]{1,0:T(8,128)(2,1)S(1)} collective-permute-done((bf16[64,2048]{1,0:T(8,128)(2,1)S(1)}, bf16[64,2048]{1,0:T(8,128)(2,1)S(1)}, u32[]{:S(2)}, u32[]{:S(2)}) %collective-permute-start.8) | collective-permute-done | bytes 262176 | tf_op jit(solution)/shard_map/ppermute | solution.py:565
  90.7 10.5 %collective-permute-done.7 = bf16[64,2048]{1,0:T(8,128)(2,1)S(1)} collective-permute-done((bf16[64,2048]{1,0:T(8,128)(2,1)S(1)}, bf16[64,2048]{1,0:T(8,128)(2,1)S(1)}, u32[]{:S(2)}, u32[]{:S(2)}) %collective-permute-start.7) | collective-permute-done | bytes 262176 | tf_op jit(solution)/shard_map/ppermute | solution.py:565
  101.2 25.5 %collective-permute-done.6 = bf16[64,2048]{1,0:T(8,128)(2,1)S(1)} collective-permute-done((bf16[64,2048]{1,0:T(8,128)(2,1)S(1)}, bf16[64,2048]{1,0:T(8,128)(2,1)S(1)}, u32[]{:S(2)}, u32[]{:S(2)}) %collective-permute-start.6) | collective-permute-done | bytes 262176 | tf_op jit(solution)/shard_map/ppermute | solution.py:565
  129.9 22.4 %collective-permute-done.15.refs_1_ = bf16[4,64,2048]{2,1,0:T(8,128)(2,1)S(1)} collective-permute-done((bf16[4,64,2048]{2,1,0:T(8,128)(2,1)S(1)}, bf16[4,64,2048]{2,1,0:T(8,128)(2,1)S(1)}, u32[]{:S(2)}, u32[]{:S(2)}) %collective-permute-start.15) | collective-permute-done | bytes 1048608 | tf_op jit(solution)/shard_map/ppermute | solution.py:565
  161.8 8.4 collective-permute-done.18
  177.7 11.5 %shard_map.229.q_raw.k_raw.v_raw.refs_4_.refs_5_ = f32[1024,1536]{1,0:T(8,128)} custom-call(bf16[1024,2048]{1,0:T(8,128)(2,1)} %bitcast.384, bf16[8,4,64,2176]{3,2,1,0:T(8,128)(2,1)} %bitcast.414), custom_call_target="tpu_custom_call" | custom-call | flops 8589934592 | tf_op jit(solution)/shard_map/pallas_call | solution.py:183
  189.2 2.7 multiply_reduce_fusion.5
  201.8 6.1 collective-permute-done.19
  208.0 12.2 %collective-permute-done.20 = f32[2,1024]{0,1:T(8,128)} collective-permute-done((f32[2,1024]{0,1:T(8,128)}, f32[2,1024]{0,1:T(8,128)}, u32[]{:S(2)}, u32[]{:S(2)}) %collective-permute-start.20) | collective-permute-done | bytes 8224 | tf_op jit(solution)/shard_map/ppermute | solution.py:575
  222.7 15.8 %shard_map.230 = (bf16[1024,512]{1,0:T(8,128)(2,1)}, bf16[1024,512]{1,0:T(8,128)(2,1)}, bf16[1024,512]{1,0:T(8,128)(2,1)}, bf16[1024,512]{1,0:T(8,128)(2,1)}) custom-call(f32[1024,1536]{1,0:T(8,128)} %shard_map.229.q_raw.k_raw.v_raw.refs_4_.refs_5_, f32[1024,1536]{1,0:T(8,128)} %shard_map.229.q_raw.k_raw.v_raw.refs_4_.refs_5_, ...), custom_call_target="tpu_custom_call" | custom-call | tf_op jit(solution)/shard_map/pallas_call | solution.py:82
  238.5 5.9 shard_map.231
  247.2 12.6 %collective-permute-done.24 = bf16[2,64,2048]{2,1,0:T(8,128)(2,1)S(1)} collective-permute-done((bf16[2,64,2048]{2,1,0:T(8,128)(2,1)}, bf16[2,64,2048]{2,1,0:T(8,128)(2,1)S(1)}, u32[]{:S(2)}, u32[]{:S(2)}) %collective-permute-start.24) | collective-permute-done | bytes 524320 | tf_op jit(solution)/shard_map/ppermute | solution.py:565
  266.3 21.2 %collective-permute-done.27 = bf16[4,64,2048]{2,1,0:T(8,128)(2,1)S(1)} collective-permute-done((bf16[4,64,2048]{2,1,0:T(8,128)(2,1)}, bf16[4,64,2048]{2,1,0:T(8,128)(2,1)S(1)}, u32[]{:S(2)}, u32[]{:S(2)}) %collective-permute-start.27) | collective-permute-done | bytes 1048608 | tf_op jit(solution)/shard_map/ppermute | solution.py:565
  290.1 4.2 fusion.24
  296.7 21.0 %collective-permute-done.28.refs_1_ = bf16[4,64,2048]{2,1,0:T(8,128)(2,1)S(1)} collective-permute-done((bf16[4,64,2048]{2,1,0:T(8,128)(2,1)S(1)}, bf16[4,64,2048]{2,1,0:T(8,128)(2,1)S(1)}, u32[]{:S(2)}, u32[]{:S(2)}) %collective-permute-start.28) | collective-permute-done | bytes 1048608 | tf_op jit(solution)/shard_map/ppermute | solution.py:565
  326.4 7.0 collective-permute-done.31
  343.5 6.8 collective-permute-done.34.refs_5_
  350.3 4.1 collective-permute-done.33.refs_4_
  355.5 5.0 all-gather.7.cloned.1.call-done
  360.5 23.7 %shard_map.233 = (bf16[1024,2048]{1,0:T(8,128)(2,1)}, f32[1024,2048]{1,0:T(8,128)}, f32[1024,2048]{1,0:T(8,128)}) custom-call(bf16[1024,2048]{1,0:T(8,128)(2,1)} %bitcast.379, bf16[8,3,4,64,2048]{4,3,2,1,0:T(8,128)(2,1)} %bitcast.370, bf16[8,3,4,64,2048]{4,3,2,1,0:T(8,128)(2,1)} %bitcast.371, bf16[64,2048]{1,0:T(8,128)(2,1)} %copy-done.49, ...), custom_call_target="tpu_custom_call" | custom-call | flops 8589934592 | tf_op jit(solution)/shard_map/pallas_call | solution.py:183
  386.4 13.2 %shard_map.234 = (bf16[2,64,2048]{2,1,0:T(8,128)(2,1)}, bf16[2,64,2048]{2,1,0:T(8,128)(2,1)}, bf16[4,64,2048]{2,1,0:T(8,128)(2,1)}, bf16[4,64,2048]{2,1,0:T(8,128)(2,1)}, bf16[4,64,2048]{2,1,0:T(8,128)(2,1)}) custom-call(s32[2]{0:T(128)} %pad_add_fusion.refs_0_, bf16[1024,2048]{1,0:T(8,128)(2,1)} %get-tuple-element.508.refs_1_, ...), custom_call_target="tpu_custom_call" | custom-call | flops 8589934592 | tf_op jit(solution)/shard_map/pallas_call | solution.py:183
  399.6 2.6 constant_dynamic-slice_fusion.10
  407.1 9.8 %collective-permute-done.37 = bf16[2,64,2048]{2,1,0:T(8,128)(2,1)} collective-permute-done((bf16[2,64,2048]{2,1,0:T(8,128)(2,1)}, bf16[2,64,2048]{2,1,0:T(8,128)(2,1)}, u32[]{:S(2)}, u32[]{:S(2)}) %collective-permute-start.37) | collective-permute-done | bytes 524320 | tf_op jit(solution)/shard_map/ppermute | solution.py:565
  421.9 9.3 %collective-permute-done.41 = bf16[64,2048]{1,0:T(8,128)(2,1)S(1)} collective-permute-done((bf16[64,2048]{1,0:T(8,128)(2,1)}, bf16[64,2048]{1,0:T(8,128)(2,1)S(1)}, u32[]{:S(2)}, u32[]{:S(2)}) %collective-permute-start.41) | collective-permute-done | bytes 262176 | tf_op jit(solution)/shard_map/ppermute | solution.py:565
  433.6 21.9 %collective-permute-done.40 = bf16[4,64,2048]{2,1,0:T(8,128)(2,1)S(1)} collective-permute-done((bf16[4,64,2048]{2,1,0:T(8,128)(2,1)S(1)}, bf16[4,64,2048]{2,1,0:T(8,128)(2,1)S(1)}, u32[]{:S(2)}, u32[]{:S(2)}) %collective-permute-start.40) | collective-permute-done | bytes 1048608 | tf_op jit(solution)/shard_map/ppermute | solution.py:565
  462.8 3.8 collective-permute-start.44
  466.5 6.8 collective-permute-done.46.refs_4_
  473.3 2.5 collective-permute-done.45.refs_3_
  475.8 7.2 collective-permute-done.44.refs_2_
  491.7 6.7 collective-permute-done.50
  502.1 17.9 %shard_map.236.refs_1_.refs_2_ = bf16[2,1024,2048]{2,1,0:T(8,128)(2,1)} custom-call(bf16[1024,2048]{1,0:T(8,128)(2,1)} %bitcast.386, bf16[8,3,4,64,2048]{4,3,2,1,0:T(8,128)(2,1)} %bitcast.373, f32[1024,2048]{1,0:T(8,128)} %get-tuple-element.551.refs_2_, f32[1024,2048]{1,0:T(8,128)} %get-tuple-element.552.refs_3_), custom_call_target="tpu_custom_call" | custom-call | flops 8589934592 | tf_op jit(solution)/shard_map/pallas_call | solution.py:183
  519.9 14.4 %shard_map.237 = bf16[4,1,256,2048]{3,2,1,0:T(8,128)(2,1)} custom-call(bf16[1024,1024]{1,0:T(8,128)(2,1)} %get-tuple-element.554.refs_0_, bf16[1024,2048]{1,0:T(8,128)(2,1)} %bitcast.387, bf16[1024,1024]{1,0:T(8,128)(2,1)} %collective-permute-done.38.refs_2_, bf16[1024,2048]{1,0:T(8,128)(2,1)} %collective-permute-done.51.refs_3_), custom_call_target="tpu_custom_call" | custom-call | flops 8589934592 | tf_op jit(solution)/shard_map/pallas_call | solution.py:183
  534.4 23.8 %shard_map.238 = (bf16[2,64,2048]{2,1,0:T(8,128)(2,1)}, bf16[2,64,2048]{2,1,0:T(8,128)(2,1)}, bf16[4,64,2048]{2,1,0:T(8,128)(2,1)}, bf16[4,64,2048]{2,1,0:T(8,128)(2,1)}, bf16[4,64,2048]{2,1,0:T(8,128)(2,1)}) custom-call(s32[2]{0:T(128)} %pad_add_fusion.refs_0_, bf16[2,1024,2048]{2,1,0:T(8,128)(2,1)} %shard_map.236.refs_1_.refs_2_, ...), custom_call_target="tpu_custom_call" | custom-call | flops 8589934592 | tf_op jit(solution)/shard_map/pallas_call | solution.py:183
  558.1 26.2 %shard_map.239 = bf16[4,2,1,4,64,2048]{5,4,3,2,1,0:T(8,128)(2,1)} custom-call(bf16[1024,1024]{1,0:T(8,128)(2,1)} %pad_maximum_fusion.4.refs_0_, bf16[2,1024,2048]{2,1,0:T(8,128)(2,1)} %shard_map.236.refs_1_.refs_2_, bf16[1024,1024]{1,0:T(8,128)(2,1)} %collective-permute-done.35.refs_2_, bf16[2,1024,2048]{2,1,0:T(8,128)(2,1)} %collective-permute-done.54.refs_3_), custom_call_target="tpu_custom_call" | custom-call | flops 8589934592 | tf_op jit(solution)/shard_map/pallas_call | solution.py:183
  587.3 11.7 %collective-permute-done.53 = bf16[2,64,2048]{2,1,0:T(8,128)(2,1)S(1)} collective-permute-done((bf16[2,64,2048]{2,1,0:T(8,128)(2,1)}, bf16[2,64,2048]{2,1,0:T(8,128)(2,1)S(1)}, u32[]{:S(2)}, u32[]{:S(2)}) %collective-permute-start.53) | collective-permute-done | bytes 524320 | tf_op jit(solution)/shard_map/ppermute | solution.py:565
  606.0 21.1 %collective-permute-done.59 = bf16[4,64,2048]{2,1,0:T(8,128)(2,1)S(1)} collective-permute-done((bf16[4,64,2048]{2,1,0:T(8,128)(2,1)S(1)}, bf16[4,64,2048]{2,1,0:T(8,128)(2,1)S(1)}, u32[]{:S(2)}, u32[]{:S(2)}) %collective-permute-start.59) | collective-permute-done | bytes 1048608 | tf_op jit(solution)/shard_map/ppermute | solution.py:565
  636.1 21.3 %collective-permute-done.60.refs_1_ = bf16[4,64,2048]{2,1,0:T(8,128)(2,1)S(1)} collective-permute-done((bf16[4,64,2048]{2,1,0:T(8,128)(2,1)S(1)}, bf16[4,64,2048]{2,1,0:T(8,128)(2,1)S(1)}, u32[]{:S(2)}, u32[]{:S(2)}) %collective-permute-start.60) | collective-permute-done | bytes 1048608 | tf_op jit(solution)/shard_map/ppermute | solution.py:565
  657.3 6.0 collective-permute-done.61.refs_0_
  670.9 6.5 collective-permute-done.63
  679.5 6.5 shard_map.241.refs_3_
  687.0 22.2 %shard_map.242 = (f32[1024,512]{1,0:T(8,128)}, f32[1024,512]{1,0:T(8,128)}, bf16[1024,512]{1,0:T(8,128)(2,1)}, f32[1024,2]{1,0:T(8,128)}, f32[1,512]{1,0:T(1,128)}, /*index=5*/f32[1,512]{1,0:T(1,128)}) custom-call(bf16[1024,512]{1,0:T(8,128)(2,1)} %get-tuple-element.613.refs_0_, bf16[1024,512]{1,0:T(8,128)(2,1)} %get-tuple-element.614.refs_1_, ...), custom_call_target="tpu_custom_call" | custom-call | tf_op jit(solution)/shard_map/pallas_call | solution.py:165
  713.9 11.4 %collective-permute-done.64 = f32[2,1024]{0,1:T(8,128)S(1)} collective-permute-done((f32[2,1024]{0,1:T(8,128)S(1)}, f32[2,1024]{0,1:T(8,128)S(1)}, u32[]{:S(2)}, u32[]{:S(2)}) %collective-permute-start.64) | collective-permute-done | bytes 8224 | tf_op jit(solution)/shard_map/ppermute | solution.py:575
  725.3 7.5 collective-permute-done.65
  738.2 10.8 %shard_map.243 = (bf16[2,64,2048]{2,1,0:T(8,128)(2,1)}, bf16[2,64,2048]{2,1,0:T(8,128)(2,1)}, bf16[4,64,2048]{2,1,0:T(8,128)(2,1)}, bf16[4,64,2048]{2,1,0:T(8,128)(2,1)}, bf16[4,64,2048]{2,1,0:T(8,128)(2,1)}) custom-call(s32[2]{0:T(128)} %pad_add_fusion.refs_0_, bf16[1024,1536]{1,0:T(8,128)(2,1)} %copy-done.32, bf16[8,4,64,2176]{3,2,1,0:T(8,128)(2,1)} %bitcast.418), custom_call_target="tpu_custom_call" | custom-call | flops 8589934592 | tf_op jit(solution)/shard_map/pallas_call | solution.py:183
  750.7 7.9 reduce-scatter.6.cloned.1.call-done
  758.6 14.9 %shard_map.244 = bf16[4,1,4,64,2048]{4,3,2,1,0:T(8,128)(2,1)} custom-call(bf16[1024,1024]{1,0:T(8,128)(2,1)} %pad_maximum_fusion.2.refs_0_, bf16[1024,1536]{1,0:T(8,128)(2,1)} %copy-done.32, bf16[1024,1024]{1,0:T(8,128)(2,1)} %collective-permute-done.22.refs_2_, bf16[1024,1536]{1,0:T(8,128)(2,1)} %collective-permute-done.69.refs_3_, ...), custom_call_target="tpu_custom_call" | custom-call | flops 8589934592 | tf_op jit(solution)/shard_map/pallas_call | solution.py:183
  781.8 20.7 %collective-permute-done.72 = bf16[4,64,2048]{2,1,0:T(8,128)(2,1)} collective-permute-done((bf16[4,64,2048]{2,1,0:T(8,128)(2,1)}, bf16[4,64,2048]{2,1,0:T(8,128)(2,1)}, u32[]{:S(2)}, u32[]{:S(2)}) %collective-permute-start.72) | collective-permute-done | bytes 1048608 | tf_op jit(solution)/shard_map/ppermute | solution.py:565
  803.8 2.5 add_convert_fusion
  815.6 3.3 collective-permute-start.75
  822.1 3.8 collective-permute-done.82
  827.6 3.6 collective-permute-done.80
  831.2 3.6 collective-permute-start.73
  835.2 7.4 collective-permute-done.74
  842.6 26.7 %collective-permute-done.73 = bf16[64,2048]{1,0:T(8,128)(2,1)S(1)} collective-permute-done((bf16[64,2048]{1,0:T(8,128)(2,1)S(1)}, bf16[64,2048]{1,0:T(8,128)(2,1)S(1)}, u32[]{:S(2)}, u32[]{:S(2)}) %collective-permute-start.73) | collective-permute-done | bytes 262176 | tf_op jit(solution)/shard_map/ppermute | solution.py:565
  880.1 7.1 collective-permute-start.91
  896.1 2.8 collective-permute-done.89
  (554 shorter events, 223.1 us)
Async XLA Ops:
  7.2 170.5 %all-gather.5.cloned.1.call-start = ((), (), s32[]{:S(2)}) async-start(), calls=%async_computation.6 | async-start | bytes 10027008 | tf_op jit(solution)/shard_map/all_gather | solution.py:745
  30.7 329.8 %all-gather.7.cloned.1.call-start = ((), (), s32[]{:S(2)}) async-start(), calls=%async_computation.7 | async-start | bytes 28311552 | tf_op jit(solution)/shard_map/all_gather | solution.py:745
  33.7 14.4 %collective-permute-start = (bf16[64,2048]{1,0:T(8,128)(2,1)S(1)}, bf16[64,2048]{1,0:T(8,128)(2,1)}, u32[]{:S(2)}, u32[]{:S(2)}) collective-permute-start(bf16[64,2048]{1,0:T(8,128)(2,1)S(1)} %copy-done.81), channel_id=1, source_target_pairs={{0,16},{16,0},{1,17},{17,1},{2,18},{18,2},{3,19},{19,3},{4,20},{20... | collective-permute-start | bytes 786440 | tf_op jit(solution)/shard_map/ppermute | solution.py:565
  34.3 34.0 %collective-permute-start.14 = (bf16[64,2048]{1,0:T(8,128)(2,1)S(1)}, bf16[64,2048]{1,0:T(8,128)(2,1)}, u32[]{:S(2)}, u32[]{:S(2)}) collective-permute-start(bf16[64,2048]{1,0:T(8,128)(2,1)S(1)} %get-tuple-element.400), channel_id=1, source_target_pairs={{0,24},{8,16},{16,8},{24,0},{1,25},{9,17},{17,9},{25,1},{2,26},{10... | collective-permute-start | bytes 786440 | tf_op jit(solution)/shard_map/ppermute | solution.py:565
  36.7 31.7 %collective-permute-start.13 = (bf16[64,2048]{1,0:T(8,128)(2,1)S(1)}, bf16[64,2048]{1,0:T(8,128)(2,1)}, u32[]{:S(2)}, u32[]{:S(2)}) collective-permute-start(bf16[64,2048]{1,0:T(8,128)(2,1)S(1)} %get-tuple-element.399), channel_id=1, source_target_pairs={{0,8},{8,0},{1,9},{9,1},{2,10},{10,2},{3,11},{11,3},{4,12},{12,4},... | collective-permute-start | bytes 786440 | tf_op jit(solution)/shard_map/ppermute | solution.py:565
  41.0 22.5 %collective-permute-start.11 = (bf16[64,2048]{1,0:T(8,128)(2,1)S(1)}, bf16[64,2048]{1,0:T(8,128)(2,1)S(1)}, u32[]{:S(2)}, u32[]{:S(2)}) collective-permute-start(bf16[64,2048]{1,0:T(8,128)(2,1)S(1)} %copy-done.80), channel_id=1, source_target_pairs={{0,24},{8,16},{16,8},{24,0},{1,25},{9,17},{17,9},{25,1},{2,26},{10... | collective-permute-start | bytes 786440 | tf_op jit(solution)/shard_map/ppermute | solution.py:565
  46.6 21.4 %collective-permute-start.10 = (bf16[64,2048]{1,0:T(8,128)(2,1)S(1)}, bf16[64,2048]{1,0:T(8,128)(2,1)S(1)}, u32[]{:S(2)}, u32[]{:S(2)}) collective-permute-start(bf16[64,2048]{1,0:T(8,128)(2,1)S(1)} %copy-done.79), channel_id=1, source_target_pairs={{0,8},{8,0},{1,9},{9,1},{2,10},{10,2},{3,11},{11,3},{4,12},{12,4},... | collective-permute-start | bytes 786440 | tf_op jit(solution)/shard_map/ppermute | solution.py:565
  48.1 19.9 %collective-permute-start.9 = (bf16[64,2048]{1,0:T(8,128)(2,1)S(1)}, bf16[64,2048]{1,0:T(8,128)(2,1)S(1)}, u32[]{:S(2)}, u32[]{:S(2)}) collective-permute-start(bf16[64,2048]{1,0:T(8,128)(2,1)S(1)} %copy-done.78), channel_id=1, source_target_pairs={{0,16},{16,0},{1,17},{17,1},{2,18},{18,2},{3,19},{19,3},{4,20},{20... | collective-permute-start | bytes 786440 | tf_op jit(solution)/shard_map/ppermute | solution.py:565
  74.0 612.1 %reduce-scatter.4.cloned.1.call-start = ((), (), s32[]{:S(2)}) async-start(), calls=%async_computation.3 | async-start | bytes 5242880 | tf_op jit(solution)/shard_map/reduce_scatter | solution.py:750
  74.1 16.6 %collective-permute-start.8 = (bf16[64,2048]{1,0:T(8,128)(2,1)S(1)}, bf16[64,2048]{1,0:T(8,128)(2,1)S(1)}, u32[]{:S(2)}, u32[]{:S(2)}) collective-permute-start(bf16[64,2048]{1,0:T(8,128)(2,1)S(1)} %get-tuple-element.389), channel_id=1, source_target_pairs={{0,3},{1,2},{2,1},{3,0},{4,7},{5,6},{6,5},{7,4},{8,11},{9,10},{10,... | collective-permute-start | bytes 786440 | tf_op jit(solution)/shard_map/ppermute | solution.py:565
  77.7 23.5 %collective-permute-start.7 = (bf16[64,2048]{1,0:T(8,128)(2,1)S(1)}, bf16[64,2048]{1,0:T(8,128)(2,1)S(1)}, u32[]{:S(2)}, u32[]{:S(2)}) collective-permute-start(bf16[64,2048]{1,0:T(8,128)(2,1)S(1)} %get-tuple-element.388), channel_id=1, source_target_pairs={{0,1},{1,0},{2,3},{3,2},{4,5},{5,4},{6,7},{7,6},{8,9},{9,8},{10,11... | collective-permute-start | bytes 786440 | tf_op jit(solution)/shard_map/ppermute | solution.py:565
  77.7 49.0 %collective-permute-start.6 = (bf16[64,2048]{1,0:T(8,128)(2,1)S(1)}, bf16[64,2048]{1,0:T(8,128)(2,1)S(1)}, u32[]{:S(2)}, u32[]{:S(2)}) collective-permute-start(bf16[64,2048]{1,0:T(8,128)(2,1)S(1)} %get-tuple-element.387), channel_id=1, source_target_pairs={{0,2},{2,0},{1,3},{3,1},{4,6},{6,4},{5,7},{7,5},{8,10},{10,8},{9,1... | collective-permute-start | bytes 786440 | tf_op jit(solution)/shard_map/ppermute | solution.py:565
  126.9 25.3 %collective-permute-start.15 = (bf16[4,64,2048]{2,1,0:T(8,128)(2,1)S(1)}, bf16[4,64,2048]{2,1,0:T(8,128)(2,1)S(1)}, u32[]{:S(2)}, u32[]{:S(2)}) collective-permute-start(bf16[4,64,2048]{2,1,0:T(8,128)(2,1)S(1)} %bitcast.388), channel_id=1, source_target_pairs={{0,8},{8,0},{1,9},{9,1},{2,10},{10,2},{3,11},{11,3},{4,12},{12,4},... | collective-permute-start | bytes 3145736 | tf_op jit(solution)/shard_map/ppermute | solution.py:565
  128.5 25.0 %collective-permute-start.16 = (bf16[4,64,2048]{2,1,0:T(8,128)(2,1)S(1)}, bf16[4,64,2048]{2,1,0:T(8,128)(2,1)S(1)}, u32[]{:S(2)}, u32[]{:S(2)}) collective-permute-start(bf16[4,64,2048]{2,1,0:T(8,128)(2,1)S(1)} %bitcast.389), channel_id=1, source_target_pairs={{0,16},{16,0},{1,17},{17,1},{2,18},{18,2},{3,19},{19,3},{4,20},{20... | collective-permute-start | bytes 3145736 | tf_op jit(solution)/shard_map/ppermute | solution.py:565
  175.0 21.4 %collective-permute-start.22 = (bf16[1024,1024]{1,0:T(8,128)(2,1)S(1)}, bf16[1024,1024]{1,0:T(8,128)(2,1)}, u32[]{:S(2)}, u32[]{:S(2)}) collective-permute-start(bf16[1024,1024]{1,0:T(8,128)(2,1)S(1)} %pad_maximum_fusion.3), channel_id=1, source_target_pairs={{0,4},{4,0},{1,5},{5,1},{2,6},{6,2},{3,7},{7,3},{8,12},{12,8},{9,1... | collective-permute-start | bytes 6291464 | tf_op jit(solution)/shard_map/ppermute | solution.py:565
  192.9 15.1 %collective-permute-start.19 = (f32[2,1024]{0,1:T(8,128)}, f32[2,1024]{0,1:T(8,128)}, u32[]{:S(2)}, u32[]{:S(2)}) collective-permute-start(f32[2,1024]{0,1:T(8,128)} %copy.92), channel_id=1, source_target_pairs={{0,8},{8,0},{1,9},{9,1},{2,10},{10,2},{3,11},{11,3},{4,12},{12,4},... | collective-permute-start | bytes 24584 | tf_op jit(solution)/shard_map/ppermute | solution.py:575
  194.4 25.8 %collective-permute-start.20 = (f32[2,1024]{0,1:T(8,128)}, f32[2,1024]{0,1:T(8,128)}, u32[]{:S(2)}, u32[]{:S(2)}) collective-permute-start(f32[2,1024]{0,1:T(8,128)} %copy.92), channel_id=1, source_target_pairs={{0,16},{16,0},{1,17},{17,1},{2,18},{18,2},{3,19},{19,3},{4,20},{20... | collective-permute-start | bytes 24584 | tf_op jit(solution)/shard_map/ppermute | solution.py:575
  195.1 25.1 %collective-permute-start.21 = (f32[2,1024]{0,1:T(8,128)}, f32[2,1024]{0,1:T(8,128)}, u32[]{:S(2)}, u32[]{:S(2)}) collective-permute-start(f32[2,1024]{0,1:T(8,128)} %copy.92), channel_id=1, source_target_pairs={{0,24},{8,16},{16,8},{24,0},{1,25},{9,17},{17,9},{25,1},{2,26},{10... | collective-permute-start | bytes 24584 | tf_op jit(solution)/shard_map/ppermute | solution.py:739
  245.3 14.5 %collective-permute-start.24 = (bf16[2,64,2048]{2,1,0:T(8,128)(2,1)}, bf16[2,64,2048]{2,1,0:T(8,128)(2,1)S(1)}, u32[]{:S(2)}, u32[]{:S(2)}) collective-permute-start(bf16[2,64,2048]{2,1,0:T(8,128)(2,1)} %get-tuple-element.453), channel_id=1, source_target_pairs={{0,16},{16,0},{1,17},{17,1},{2,18},{18,2},{3,19},{19,3},{4,20},{20... | collective-permute-start | bytes 1572872 | tf_op jit(solution)/shard_map/ppermute | solution.py:565
  245.8 14.3 %collective-permute-start.23 = (bf16[2,64,2048]{2,1,0:T(8,128)(2,1)}, bf16[2,64,2048]{2,1,0:T(8,128)(2,1)S(1)}, u32[]{:S(2)}, u32[]{:S(2)}) collective-permute-start(bf16[2,64,2048]{2,1,0:T(8,128)(2,1)} %get-tuple-element.452), channel_id=1, source_target_pairs={{0,8},{8,0},{1,9},{9,1},{2,10},{10,2},{3,11},{11,3},{4,12},{12,4},... | collective-permute-start | bytes 1572872 | tf_op jit(solution)/shard_map/ppermute | solution.py:565
  262.5 24.9 %collective-permute-start.27 = (bf16[4,64,2048]{2,1,0:T(8,128)(2,1)}, bf16[4,64,2048]{2,1,0:T(8,128)(2,1)S(1)}, u32[]{:S(2)}, u32[]{:S(2)}) collective-permute-start(bf16[4,64,2048]{2,1,0:T(8,128)(2,1)} %pad_maximum_fusion.8), channel_id=1, source_target_pairs={{0,8},{8,0},{1,9},{9,1},{2,10},{10,2},{3,11},{11,3},{4,12},{12,4},... | collective-permute-start | bytes 3145736 | tf_op jit(solution)/shard_map/ppermute | solution.py:565
  263.7 24.6 %collective-permute-start.26 = (bf16[4,64,2048]{2,1,0:T(8,128)(2,1)}, bf16[4,64,2048]{2,1,0:T(8,128)(2,1)}, u32[]{:S(2)}, u32[]{:S(2)}) collective-permute-start(bf16[4,64,2048]{2,1,0:T(8,128)(2,1)} %pad_maximum_fusion.7), channel_id=1, source_target_pairs={{0,16},{16,0},{1,17},{17,1},{2,18},{18,2},{3,19},{19,3},{4,20},{20... | collective-permute-start | bytes 3145736 | tf_op jit(solution)/shard_map/ppermute | solution.py:565
  294.3 23.4 %collective-permute-start.28 = (bf16[4,64,2048]{2,1,0:T(8,128)(2,1)S(1)}, bf16[4,64,2048]{2,1,0:T(8,128)(2,1)S(1)}, u32[]{:S(2)}, u32[]{:S(2)}) collective-permute-start(bf16[4,64,2048]{2,1,0:T(8,128)(2,1)S(1)} %get-tuple-element.472), channel_id=1, source_target_pairs={{0,8},{8,0},{1,9},{9,1},{2,10},{10,2},{3,11},{11,3},{4,12},{12,4},... | collective-permute-start | bytes 3145736 | tf_op jit(solution)/shard_map/ppermute | solution.py:565
  295.3 23.2 %collective-permute-start.29 = (bf16[4,64,2048]{2,1,0:T(8,128)(2,1)S(1)}, bf16[4,64,2048]{2,1,0:T(8,128)(2,1)S(1)}, u32[]{:S(2)}, u32[]{:S(2)}) collective-permute-start(bf16[4,64,2048]{2,1,0:T(8,128)(2,1)S(1)} %get-tuple-element.472), channel_id=1, source_target_pairs={{0,16},{16,0},{1,17},{17,1},{2,18},{18,2},{3,19},{19,3},{4,20},{20... | collective-permute-start | bytes 3145736 | tf_op jit(solution)/shard_map/ppermute | solution.py:565
  340.0 15.5 %collective-permute-start.35 = (bf16[1024,1024]{1,0:T(8,128)(2,1)}, bf16[1024,1024]{1,0:T(8,128)(2,1)}, u32[]{:S(2)}, u32[]{:S(2)}) collective-permute-start(bf16[1024,1024]{1,0:T(8,128)(2,1)} %pad_maximum_fusion.5), channel_id=1, source_target_pairs={{0,4},{4,0},{1,5},{5,1},{2,6},{6,2},{3,7},{7,3},{8,12},{12,8},{9,1... | collective-permute-start | bytes 6291464 | tf_op jit(solution)/shard_map/ppermute | solution.py:565
  402.2 15.8 %collective-permute-start.38 = (bf16[1024,1024]{1,0:T(8,128)(2,1)}, bf16[1024,1024]{1,0:T(8,128)(2,1)}, u32[]{:S(2)}, u32[]{:S(2)}) collective-permute-start(bf16[1024,1024]{1,0:T(8,128)(2,1)} %get-tuple-element.509), channel_id=1, source_target_pairs={{0,4},{4,0},{1,5},{5,1},{2,6},{6,2},{3,7},{7,3},{8,12},{12,8},{9,1... | collective-permute-start | bytes 6291464 | tf_op jit(solution)/shard_map/ppermute | solution.py:565
  402.5 14.4 %collective-permute-start.37 = (bf16[2,64,2048]{2,1,0:T(8,128)(2,1)}, bf16[2,64,2048]{2,1,0:T(8,128)(2,1)}, u32[]{:S(2)}, u32[]{:S(2)}) collective-permute-start(bf16[2,64,2048]{2,1,0:T(8,128)(2,1)} %get-tuple-element.507), channel_id=1, source_target_pairs={{0,16},{16,0},{1,17},{17,1},{2,18},{18,2},{3,19},{19,3},{4,20},{20... | collective-permute-start | bytes 1572872 | tf_op jit(solution)/shard_map/ppermute | solution.py:565
  405.8 16.1 %collective-permute-start.43 = (bf16[64,2048]{1,0:T(8,128)(2,1)}, bf16[64,2048]{1,0:T(8,128)(2,1)S(1)}, u32[]{:S(2)}, u32[]{:S(2)}) collective-permute-start(bf16[64,2048]{1,0:T(8,128)(2,1)} %get-tuple-element.518), channel_id=1, source_target_pairs={{0,3},{1,2},{2,1},{3,0},{4,7},{5,6},{6,5},{7,4},{8,11},{9,10},{10,... | collective-permute-start | bytes 786440 | tf_op jit(solution)/shard_map/ppermute | solution.py:565
  406.4 15.5 %collective-permute-start.42 = (bf16[64,2048]{1,0:T(8,128)(2,1)}, bf16[64,2048]{1,0:T(8,128)(2,1)S(1)}, u32[]{:S(2)}, u32[]{:S(2)}) collective-permute-start(bf16[64,2048]{1,0:T(8,128)(2,1)} %get-tuple-element.517), channel_id=1, source_target_pairs={{0,1},{1,0},{2,3},{3,2},{4,5},{5,4},{6,7},{7,6},{8,9},{9,8},{10,11... | collective-permute-start | bytes 786440 | tf_op jit(solution)/shard_map/ppermute | solution.py:565
  416.9 14.4 %collective-permute-start.41 = (bf16[64,2048]{1,0:T(8,128)(2,1)}, bf16[64,2048]{1,0:T(8,128)(2,1)S(1)}, u32[]{:S(2)}, u32[]{:S(2)}) collective-permute-start(bf16[64,2048]{1,0:T(8,128)(2,1)} %get-tuple-element.516), channel_id=1, source_target_pairs={{0,2},{2,0},{1,3},{3,1},{4,6},{6,4},{5,7},{7,5},{8,10},{10,8},{9,1... | collective-permute-start | bytes 786440 | tf_op jit(solution)/shard_map/ppermute | solution.py:565
  431.2 24.3 %collective-permute-start.40 = (bf16[4,64,2048]{2,1,0:T(8,128)(2,1)S(1)}, bf16[4,64,2048]{2,1,0:T(8,128)(2,1)S(1)}, u32[]{:S(2)}, u32[]{:S(2)}) collective-permute-start(bf16[4,64,2048]{2,1,0:T(8,128)(2,1)S(1)} %pad_maximum_fusion.10), channel_id=1, source_target_pairs={{0,8},{8,0},{1,9},{9,1},{2,10},{10,2},{3,11},{11,3},{4,12},{12,4},... | collective-permute-start | bytes 3145736 | tf_op jit(solution)/shard_map/ppermute | solution.py:565
  432.3 24.1 %collective-permute-start.39 = (bf16[4,64,2048]{2,1,0:T(8,128)(2,1)S(1)}, bf16[4,64,2048]{2,1,0:T(8,128)(2,1)S(1)}, u32[]{:S(2)}, u32[]{:S(2)}) collective-permute-start(bf16[4,64,2048]{2,1,0:T(8,128)(2,1)S(1)} %pad_maximum_fusion.9), channel_id=1, source_target_pairs={{0,16},{16,0},{1,17},{17,1},{2,18},{18,2},{3,19},{19,3},{4,20},{20... | collective-permute-start | bytes 3145736 | tf_op jit(solution)/shard_map/ppermute | solution.py:565
  459.9 23.2 %collective-permute-start.47 = (bf16[4,64,2048]{2,1,0:T(8,128)(2,1)S(1)}, bf16[4,64,2048]{2,1,0:T(8,128)(2,1)S(1)}, u32[]{:S(2)}, u32[]{:S(2)}) collective-permute-start(bf16[4,64,2048]{2,1,0:T(8,128)(2,1)S(1)} %get-tuple-element.541), channel_id=1, source_target_pairs={{0,8},{8,0},{1,9},{9,1},{2,10},{10,2},{3,11},{11,3},{4,12},{12,4},... | collective-permute-start | bytes 3145736 | tf_op jit(solution)/shard_map/ppermute | solution.py:565
  460.8 22.8 %collective-permute-start.48 = (bf16[4,64,2048]{2,1,0:T(8,128)(2,1)S(1)}, bf16[4,64,2048]{2,1,0:T(8,128)(2,1)S(1)}, u32[]{:S(2)}, u32[]{:S(2)}) collective-permute-start(bf16[4,64,2048]{2,1,0:T(8,128)(2,1)S(1)} %get-tuple-element.541), channel_id=1, source_target_pairs={{0,16},{16,0},{1,17},{17,1},{2,18},{18,2},{3,19},{19,3},{4,20},{20... | collective-permute-start | bytes 3145736 | tf_op jit(solution)/shard_map/ppermute | solution.py:565
  462.8 20.2 %collective-permute-start.44 = (bf16[64,2048]{1,0:T(8,128)(2,1)S(1)}, bf16[64,2048]{1,0:T(8,128)(2,1)S(1)}, u32[]{:S(2)}, u32[]{:S(2)}) collective-permute-start(bf16[64,2048]{1,0:T(8,128)(2,1)S(1)} %get-tuple-element.530), channel_id=1, source_target_pairs={{0,2},{2,0},{1,3},{3,1},{4,6},{6,4},{5,7},{7,5},{8,10},{10,8},{9,1... | collective-permute-start | bytes 786440 | tf_op jit(solution)/shard_map/ppermute | solution.py:565
  500.0 19.9 %collective-permute-start.51 = (bf16[1024,2048]{1,0:T(8,128)(2,1)S(1)}, bf16[1024,2048]{1,0:T(8,128)(2,1)}, u32[]{:S(2)}, u32[]{:S(2)}) collective-permute-start(bf16[1024,2048]{1,0:T(8,128)(2,1)S(1)} %bitcast.385), channel_id=1, source_target_pairs={{0,4},{4,0},{1,5},{5,1},{2,6},{6,2},{3,7},{7,3},{8,12},{12,8},{9,1... | collective-permute-start | bytes 12582920 | tf_op jit(solution)/shard_map/ppermute | solution.py:565
  519.9 38.2 %collective-permute-start.54 = (bf16[2,1024,2048]{2,1,0:T(8,128)(2,1)}, bf16[2,1024,2048]{2,1,0:T(8,128)(2,1)}, u32[]{:S(2)}, u32[]{:S(2)}) collective-permute-start(bf16[2,1024,2048]{2,1,0:T(8,128)(2,1)} %shard_map.236.refs_1_.refs_2_), channel_id=1, source_target_pairs={{0,4},{4,0},{1,5},{5,1},{2,6},{6,2},{3,7},{7,3},{8,12},{12,8},{9,1... | collective-permute-start | bytes 25165832 | tf_op jit(solution)/shard_map/ppermute | solution.py:565
  534.3 224.3 %reduce-scatter.6.cloned.1.call-start = ((), (), s32[]{:S(2)}) async-start(), calls=%async_computation.4 | async-start | bytes 10485760 | tf_op jit(solution)/shard_map/reduce_scatter | solution.py:750
  584.4 291.0 %reduce-scatter.8.cloned.1.call-start = ((), (), s32[]{:S(2)}) async-start(), calls=%async_computation.5 | async-start | bytes 5242880 | tf_op jit(solution)/shard_map/reduce_scatter | solution.py:750
  584.4 14.6 %collective-permute-start.53 = (bf16[2,64,2048]{2,1,0:T(8,128)(2,1)}, bf16[2,64,2048]{2,1,0:T(8,128)(2,1)S(1)}, u32[]{:S(2)}, u32[]{:S(2)}) collective-permute-start(bf16[2,64,2048]{2,1,0:T(8,128)(2,1)} %get-tuple-element.567), channel_id=1, source_target_pairs={{0,16},{16,0},{1,17},{17,1},{2,18},{18,2},{3,19},{19,3},{4,20},{20... | collective-permute-start | bytes 1572872 | tf_op jit(solution)/shard_map/ppermute | solution.py:565
  602.6 24.6 %collective-permute-start.59 = (bf16[4,64,2048]{2,1,0:T(8,128)(2,1)S(1)}, bf16[4,64,2048]{2,1,0:T(8,128)(2,1)S(1)}, u32[]{:S(2)}, u32[]{:S(2)}) collective-permute-start(bf16[4,64,2048]{2,1,0:T(8,128)(2,1)S(1)} %pad_maximum_fusion.12), channel_id=1, source_target_pairs={{0,8},{8,0},{1,9},{9,1},{2,10},{10,2},{3,11},{11,3},{4,12},{12,4},... | collective-permute-start | bytes 3145736 | tf_op jit(solution)/shard_map/ppermute | solution.py:565
  604.4 24.2 %collective-permute-start.58 = (bf16[4,64,2048]{2,1,0:T(8,128)(2,1)S(1)}, bf16[4,64,2048]{2,1,0:T(8,128)(2,1)S(1)}, u32[]{:S(2)}, u32[]{:S(2)}) collective-permute-start(bf16[4,64,2048]{2,1,0:T(8,128)(2,1)S(1)} %pad_maximum_fusion.11), channel_id=1, source_target_pairs={{0,16},{16,0},{1,17},{17,1},{2,18},{18,2},{3,19},{19,3},{4,20},{20... | collective-permute-start | bytes 3145736 | tf_op jit(solution)/shard_map/ppermute | solution.py:565
  631.2 26.1 %collective-permute-start.60 = (bf16[4,64,2048]{2,1,0:T(8,128)(2,1)S(1)}, bf16[4,64,2048]{2,1,0:T(8,128)(2,1)S(1)}, u32[]{:S(2)}, u32[]{:S(2)}) collective-permute-start(bf16[4,64,2048]{2,1,0:T(8,128)(2,1)S(1)} %multiply_convert_fusion.2), channel_id=1, source_target_pairs={{0,8},{8,0},{1,9},{9,1},{2,10},{10,2},{3,11},{11,3},{4,12},{12,4},... | collective-permute-start | bytes 3145736 | tf_op jit(solution)/shard_map/ppermute | solution.py:565
  631.6 31.7 %collective-permute-start.61 = (bf16[4,64,2048]{2,1,0:T(8,128)(2,1)S(1)}, bf16[4,64,2048]{2,1,0:T(8,128)(2,1)S(1)}, u32[]{:S(2)}, u32[]{:S(2)}) collective-permute-start(bf16[4,64,2048]{2,1,0:T(8,128)(2,1)S(1)} %multiply_convert_fusion.2), channel_id=1, source_target_pairs={{0,16},{16,0},{1,17},{17,1},{2,18},{18,2},{3,19},{19,3},{4,20},{20... | collective-permute-start | bytes 3145736 | tf_op jit(solution)/shard_map/ppermute | solution.py:565
  632.6 53.5 %collective-permute-start.57 = (bf16[64,2048]{1,0:T(8,128)(2,1)}, bf16[64,2048]{1,0:T(8,128)(2,1)S(1)}, u32[]{:S(2)}, u32[]{:S(2)}) collective-permute-start(bf16[64,2048]{1,0:T(8,128)(2,1)} %get-tuple-element.583), channel_id=1, source_target_pairs={{0,24},{8,16},{16,8},{24,0},{1,25},{9,17},{17,9},{25,1},{2,26},{10... | collective-permute-start | bytes 786440 | tf_op jit(solution)/shard_map/ppermute | solution.py:565
  634.7 51.4 %collective-permute-start.56 = (bf16[64,2048]{1,0:T(8,128)(2,1)}, bf16[64,2048]{1,0:T(8,128)(2,1)S(1)}, u32[]{:S(2)}, u32[]{:S(2)}) collective-permute-start(bf16[64,2048]{1,0:T(8,128)(2,1)} %get-tuple-element.582), channel_id=1, source_target_pairs={{0,8},{8,0},{1,9},{9,1},{2,10},{10,2},{3,11},{11,3},{4,12},{12,4},... | collective-permute-start | bytes 786440 | tf_op jit(solution)/shard_map/ppermute | solution.py:565
  635.1 51.0 %collective-permute-start.55 = (bf16[64,2048]{1,0:T(8,128)(2,1)}, bf16[64,2048]{1,0:T(8,128)(2,1)S(1)}, u32[]{:S(2)}, u32[]{:S(2)}) collective-permute-start(bf16[64,2048]{1,0:T(8,128)(2,1)} %get-tuple-element.581), channel_id=1, source_target_pairs={{0,16},{16,0},{1,17},{17,1},{2,18},{18,2},{3,19},{19,3},{4,20},{20... | collective-permute-start | bytes 786440 | tf_op jit(solution)/shard_map/ppermute | solution.py:565
  710.3 14.9 %collective-permute-start.64 = (f32[2,1024]{0,1:T(8,128)S(1)}, f32[2,1024]{0,1:T(8,128)S(1)}, u32[]{:S(2)}, u32[]{:S(2)}) collective-permute-start(f32[2,1024]{0,1:T(8,128)S(1)} %multiply_bitcast_fusion), channel_id=1, source_target_pairs={{0,8},{8,0},{1,9},{9,1},{2,10},{10,2},{3,11},{11,3},{4,12},{12,4},... | collective-permute-start | bytes 24584 | tf_op jit(solution)/shard_map/ppermute | solution.py:575
  711.9 20.9 %collective-permute-start.65 = (f32[2,1024]{0,1:T(8,128)S(1)}, f32[2,1024]{0,1:T(8,128)S(1)}, u32[]{:S(2)}, u32[]{:S(2)}) collective-permute-start(f32[2,1024]{0,1:T(8,128)S(1)} %multiply_bitcast_fusion), channel_id=1, source_target_pairs={{0,16},{16,0},{1,17},{17,1},{2,18},{18,2},{3,19},{19,3},{4,20},{20... | collective-permute-start | bytes 24584 | tf_op jit(solution)/shard_map/ppermute | solution.py:575
  712.8 19.9 %collective-permute-start.66 = (f32[2,1024]{0,1:T(8,128)S(1)}, f32[2,1024]{0,1:T(8,128)S(1)}, u32[]{:S(2)}, u32[]{:S(2)}) collective-permute-start(f32[2,1024]{0,1:T(8,128)S(1)} %multiply_bitcast_fusion), channel_id=1, source_target_pairs={{0,24},{8,16},{16,8},{24,0},{1,25},{9,17},{17,9},{25,1},{2,26},{10... | collective-permute-start | bytes 24584 | tf_op jit(solution)/shard_map/ppermute | solution.py:739
  713.9 36.8 %collective-permute-start.70 = (bf16[1024,2048]{1,0:T(8,128)(2,1)}, bf16[1024,2048]{1,0:T(8,128)(2,1)}, u32[]{:S(2)}, u32[]{:S(2)}) collective-permute-start(bf16[1024,2048]{1,0:T(8,128)(2,1)} %bitcast.397), channel_id=1, source_target_pairs={{0,4},{4,0},{1,5},{5,1},{2,6},{6,2},{3,7},{7,3},{8,12},{12,8},{9,1... | collective-permute-start | bytes 12582920 | tf_op jit(solution)/shard_map/ppermute | solution.py:575
  736.5 14.2 %collective-permute-start.69 = (bf16[1024,1536]{1,0:T(8,128)(2,1)S(1)}, bf16[1024,1536]{1,0:T(8,128)(2,1)}, u32[]{:S(2)}, u32[]{:S(2)}) collective-permute-start(bf16[1024,1536]{1,0:T(8,128)(2,1)S(1)} %pad_maximum_fusion.1.refs_1_), channel_id=1, source_target_pairs={{0,4},{4,0},{1,5},{5,1},{2,6},{6,2},{3,7},{7,3},{8,12},{12,8},{9,1... | collective-permute-start | bytes 9437192 | tf_op jit(solution)/shard_map/ppermute | solution.py:575
  748.9 24.6 %collective-permute-start.68 = (bf16[2,64,2048]{2,1,0:T(8,128)(2,1)}, bf16[2,64,2048]{2,1,0:T(8,128)(2,1)}, u32[]{:S(2)}, u32[]{:S(2)}) collective-permute-start(bf16[2,64,2048]{2,1,0:T(8,128)(2,1)} %get-tuple-element.649), channel_id=1, source_target_pairs={{0,16},{16,0},{1,17},{17,1},{2,18},{18,2},{3,19},{19,3},{4,20},{20... | collective-permute-start | bytes 1572872 | tf_op jit(solution)/shard_map/ppermute | solution.py:565
  749.9 23.6 %collective-permute-start.67 = (bf16[2,64,2048]{2,1,0:T(8,128)(2,1)}, bf16[2,64,2048]{2,1,0:T(8,128)(2,1)}, u32[]{:S(2)}, u32[]{:S(2)}) collective-permute-start(bf16[2,64,2048]{2,1,0:T(8,128)(2,1)} %get-tuple-element.648), channel_id=1, source_target_pairs={{0,8},{8,0},{1,9},{9,1},{2,10},{10,2},{3,11},{11,3},{4,12},{12,4},... | collective-permute-start | bytes 1572872 | tf_op jit(solution)/shard_map/ppermute | solution.py:565
  777.3 25.1 %collective-permute-start.72 = (bf16[4,64,2048]{2,1,0:T(8,128)(2,1)}, bf16[4,64,2048]{2,1,0:T(8,128)(2,1)}, u32[]{:S(2)}, u32[]{:S(2)}) collective-permute-start(bf16[4,64,2048]{2,1,0:T(8,128)(2,1)} %pad_maximum_fusion.14), channel_id=1, source_target_pairs={{0,8},{8,0},{1,9},{9,1},{2,10},{10,2},{3,11},{11,3},{4,12},{12,4},... | collective-permute-start | bytes 3145736 | tf_op jit(solution)/shard_map/ppermute | solution.py:565
  778.9 24.9 %collective-permute-start.71 = (bf16[4,64,2048]{2,1,0:T(8,128)(2,1)S(1)}, bf16[4,64,2048]{2,1,0:T(8,128)(2,1)}, u32[]{:S(2)}, u32[]{:S(2)}) collective-permute-start(bf16[4,64,2048]{2,1,0:T(8,128)(2,1)S(1)} %pad_maximum_fusion.13), channel_id=1, source_target_pairs={{0,16},{16,0},{1,17},{17,1},{2,18},{18,2},{3,19},{19,3},{4,20},{20... | collective-permute-start | bytes 3145736 | tf_op jit(solution)/shard_map/ppermute | solution.py:565
  781.1 25.3 %collective-permute-start.76 = (f32[4,2,2,2,2,64]{5,4,3,0,2,1:T(2,128)S(1)}, f32[4,2,2,2,2,64]{5,4,3,0,2,1:T(2,128)S(1)}, u32[]{:S(2)}, u32[]{:S(2)}) collective-permute-start(f32[4,2,2,2,2,64]{5,4,3,0,2,1:T(2,128)S(1)} %get-tuple-element.675), channel_id=1, source_target_pairs={{0,16},{16,0},{1,17},{17,1},{2,18},{18,2},{3,19},{19,3},{4,20},{20... | collective-permute-start | bytes 49160 | tf_op jit(solution)/shard_map/ppermute | solution.py:565
  815.6 19.6 %collective-permute-start.75 = (bf16[64,2048]{1,0:T(8,128)(2,1)S(1)}, bf16[64,2048]{1,0:T(8,128)(2,1)S(1)}, u32[]{:S(2)}, u32[]{:S(2)}) collective-permute-start(bf16[64,2048]{1,0:T(8,128)(2,1)S(1)} %get-tuple-element.674), channel_id=1, source_target_pairs={{0,3},{1,2},{2,1},{3,0},{4,7},{5,6},{6,5},{7,4},{8,11},{9,10},{10,... | collective-permute-start | bytes 786440 | tf_op jit(solution)/shard_map/ppermute | solution.py:565
  818.8 23.7 %collective-permute-start.74 = (bf16[64,2048]{1,0:T(8,128)(2,1)S(1)}, bf16[64,2048]{1,0:T(8,128)(2,1)S(1)}, u32[]{:S(2)}, u32[]{:S(2)}) collective-permute-start(bf16[64,2048]{1,0:T(8,128)(2,1)S(1)} %get-tuple-element.673), channel_id=1, source_target_pairs={{0,1},{1,0},{2,3},{3,2},{4,5},{5,4},{6,7},{7,6},{8,9},{9,8},{10,11... | collective-permute-start | bytes 786440 | tf_op jit(solution)/shard_map/ppermute | solution.py:565
  831.2 38.0 %collective-permute-start.73 = (bf16[64,2048]{1,0:T(8,128)(2,1)S(1)}, bf16[64,2048]{1,0:T(8,128)(2,1)S(1)}, u32[]{:S(2)}, u32[]{:S(2)}) collective-permute-start(bf16[64,2048]{1,0:T(8,128)(2,1)S(1)} %get-tuple-element.672), channel_id=1, source_target_pairs={{0,2},{2,0},{1,3},{3,1},{4,6},{6,4},{5,7},{7,5},{8,10},{10,8},{9,1... | collective-permute-start | bytes 786440 | tf_op jit(solution)/shard_map/ppermute | solution.py:565
  834.8 42.6 %collective-permute-start.87 = (f32[4,2,2,64]{3,2,1,0:T(2,128)S(1)}, f32[4,2,2,64]{3,2,1,0:T(2,128)S(1)}, u32[]{:S(2)}, u32[]{:S(2)}) collective-permute-start(f32[4,2,2,64]{3,2,1,0:T(2,128)S(1)} %get-tuple-element.704), channel_id=1, source_target_pairs={{0,4},{4,0},{1,5},{5,1},{2,6},{6,2},{3,7},{7,3},{8,12},{12,8},{9,1... | collective-permute-start | bytes 12296 | tf_op jit(solution)/shard_map/ppermute | solution.py:565
  869.6 20.9 %collective-permute-start.86 = (bf16[64,2048]{1,0:T(8,128)(2,1)S(1)}, bf16[64,2048]{1,0:T(8,128)(2,1)S(1)}, u32[]{:S(2)}, u32[]{:S(2)}) collective-permute-start(bf16[64,2048]{1,0:T(8,128)(2,1)S(1)} %get-tuple-element.703), channel_id=1, source_target_pairs={{0,24},{8,16},{16,8},{24,0},{1,25},{9,17},{17,9},{25,1},{2,26},{10... | collective-permute-start | bytes 786440 | tf_op jit(solution)/shard_map/ppermute | solution.py:565
  871.5 19.6 %collective-permute-start.85 = (bf16[64,2048]{1,0:T(8,128)(2,1)S(1)}, bf16[64,2048]{1,0:T(8,128)(2,1)S(1)}, u32[]{:S(2)}, u32[]{:S(2)}) collective-permute-start(bf16[64,2048]{1,0:T(8,128)(2,1)S(1)} %get-tuple-element.702), channel_id=1, source_target_pairs={{0,8},{8,0},{1,9},{9,1},{2,10},{10,2},{3,11},{11,3},{4,12},{12,4},... | collective-permute-start | bytes 786440 | tf_op jit(solution)/shard_map/ppermute | solution.py:565
  872.6 19.1 %collective-permute-start.84 = (bf16[64,2048]{1,0:T(8,128)(2,1)S(1)}, bf16[64,2048]{1,0:T(8,128)(2,1)S(1)}, u32[]{:S(2)}, u32[]{:S(2)}) collective-permute-start(bf16[64,2048]{1,0:T(8,128)(2,1)S(1)} %get-tuple-element.701), channel_id=1, source_target_pairs={{0,16},{16,0},{1,17},{17,1},{2,18},{18,2},{3,19},{19,3},{4,20},{20... | collective-permute-start | bytes 786440 | tf_op jit(solution)/shard_map/ppermute | solution.py:565
  (124 other events, 1056.2 us)
Sparse Core Ops, SparseCore 0:
  30.8 109.7 all-gather.4
  142.2 218.2 all-gather.6
  534.4 76.8 reduce-scatter.3
  613.6 144.9 reduce-scatter.5
  781.9 93.4 reduce-scatter.7
where the time goes:
time: 915 us; the launch traced here: 907 us
  waiting for transfers between devices  447 us (49%)
  Pallas kernels  217 us (24%)
  starting transfers between devices  109 us (12%)
  local copies, waits for them, and re-layouts  68.6 us (7%)
  other arithmetic  50 us (5%)
  between operations  16.4 us (2%)
    ppermute x85, waiting for transfers between devices, send(): return lax.ppermute(value, axes, pairs)  394 us
    pallas_call x16, Pallas kernels, call(): pl.pallas_call(body, grid=grid, in_specs=[spec for _, spec in scalars] +...  179 us
    ppermute x85, starting transfers between devices, send(): return lax.ppermute(value, axes, pairs)  101 us
    ppermute x6, waiting for transfers between devices, swap(): return lax.ppermute(value, axis, SWAP)  37.3 us
    unnamed x181, local copies, waits for them, and re-layouts  22.9 us
    pallas_call x1, Pallas kernels, attend_back(): pl.pallas_call(body, grid=(heads,), in_specs=[column(0)] * 4 + [column(0)...  22.2 us
  transfers between devices with their start and end apart: 98, of which 62 were waited for; matrix products, arithmetic and copies ran while one was open for 8% of the time, Pallas kernels for 20%

commit v1 on v0

--- a/solution.py
+++ b/solution.py
@@ -401,29 +401,33 @@
     )
 
 
-def down_grad(hidden, branch_rows, groups, rows):
+def down_grad(core, hidden, branch_rows, groups, rows):
     length, units = hidden[0].shape
     width = branch_rows[0].shape[1]
     run = 4 * rows
     many = 1 if run % 128 == 0 else 4
     shape = (4, groups, run, width)
 
-    def kernel(a, b, c, d, out):
+    def kernel(core, a, b, c, d, out):
         total = dot_tn(a[...], b[...]) + dot_tn(c[...], d[...])
         out[...] = total.astype(LOW).reshape(out.shape)
 
-    cut = ((length, many * run), lambda g, j: (0, g * (4 // many) + j))
-    return call(
+    cut = pl.BlockSpec(
+        (length, many * run), lambda g, j, core: (0, (g * 2 + core[0]) * (4 // many) + j)
+    )
+    whole = pl.BlockSpec((length, width), lambda g, j, core: (0, 0))
+    return pl.pallas_call(
         kernel,
-        (groups, 4 // many),
-        [
-            (hidden[0],) + cut,
-            stay(branch_rows[0]),
-            (hidden[1],) + cut,
-            stay(branch_rows[1]),
-        ],
-        [(shape, LOW, (many, 1, run, width), lambda g, j: (j, g, 0, 0))],
-    )
+        grid_spec=pltpu.PrefetchScalarGridSpec(
+            num_scalar_prefetch=1,
+            grid=(groups, 4 // many),
+            in_specs=[cut, whole, cut, whole],
+            out_specs=pl.BlockSpec((many, 1, run, width), lambda g, j, core: (j, g, 0, 0)),
+        ),
+        out_shape=jax.ShapeDtypeStruct(shape, LOW),
+        compiler_params=pltpu.CompilerParams(vmem_limit_bytes=VMEM_LIMIT),
+        cost_estimate=pl.CostEstimate(flops=2**33, bytes_accessed=0, transcendentals=0),
+    )(core, hidden[0], branch_rows[0], hidden[1], branch_rows[1])
 
 
 def lay_features(total, out, many, rows):
@@ -977,8 +981,7 @@
     hidden, gate_raw, up_raw = steps(gated, mlp_in, mlp_all, top.spread.came)
     top.second()
     branch = ScatterTokens(at, branch_out, places, hidden, mlp_all)
-    hidden_half = pair(*steps(lambda v: halves(v, at.c, groups), hidden))
-    steps.wait(hidden_half)
+    hidden = (hidden, at.links.swap(hidden, "c"))
     branch.second()
     own_top = top.third()
 
@@ -998,11 +1001,14 @@
     branch_rows = (branch_rows, at.links.swap(branch_rows, "c"))
     unit_grads = steps(gated_back, branch_rows[0], mlp_all, gate_raw, up_raw)
     unit_grads = (unit_grads, at.links.swap(unit_grads, "c"))
-    grad = steps(lambda a, b: down_grad(a, b, groups, rows_owned), hidden_half, branch_rows)
+    core = at.c.astype(jnp.int32).reshape(1)
+    grad = steps(
+        lambda *v: down_grad(*v, groups, rows_owned), core, hidden, branch_rows
+    )
     down_own = scatter(at, grad)
-    input_part = ScatterTokens(at, input_back, places, unit_grads[0], mlp_all)
     grad = steps(lambda a, b: units_grad(a, b, groups, rows_owned), mlp_in_half, unit_grads)
     units_own = scatter(at, grad)
+    input_part = ScatterTokens(at, input_back, places, unit_grads[0], mlp_all)
     input_part.second()
     layer_out.second()
     layer_out_came = layer_out.spread.came

time: 915 us -> 909 us (level)
    pallas_call x0 -> x1, Pallas kernels: none -> 14.4 us  [down_grad(): pl.pallas_call(kernel, grid_spec=pltpu.PrefetchScalarGridSpec(num_scalar_...]
    pallas_call x16 -> x15, Pallas kernels: 179 us -> 165 us  [call(): pl.pallas_call(body, grid=grid, in_specs=[spec for _, spec in scalars] +...]
    unnamed x181 -> x183, local copies, waits for them, and re-layouts: 22.9 us -> 23.5 us
where the time goes in v1:
time: 909 us; the launch traced here: 901 us
  waiting for transfers between devices  443 us (49%)
  Pallas kernels  218 us (24%)
  starting transfers between devices  109 us (12%)
  local copies, waits for them, and re-layouts  66.6 us (7%)
  other arithmetic  48.7 us (5%)
  between operations  16.2 us (2%)
    ppermute x85, waiting for transfers between devices, send(): return lax.ppermute(value, axes, pairs)  392 us
    pallas_call x15, Pallas kernels, call(): pl.pallas_call(body, grid=grid, in_specs=[spec for _, spec in scalars] +...  165 us
    ppermute x85, starting transfers between devices, send(): return lax.ppermute(value, axes, pairs)  102 us
    ppermute x6, waiting for transfers between devices, swap(): return lax.ppermute(value, axis, SWAP)  36.4 us
    unnamed x183, local copies, waits for them, and re-layouts  23.5 us
    pallas_call x1, Pallas kernels, attend_back(): pl.pallas_call(body, grid=(heads,), in_specs=[column(0)] * 4 + [column(0)...  22.8 us
  transfers between devices with their start and end apart: 98, of which 62 were waited for; matrix products, arithmetic and copies ran while one was open for 8% of the time, Pallas kernels for 20%

profile of v1, /device:TPU:0, one launch (start us, length us, event | category | flops | bytes accessed | tf_op | source)
XLA Modules:
  0.0 901.1 jit_solution(1260662196130776565)
XLA Ops:
  12.1 3.9 collective-permute-start.5
  18.6 3.8 collective-permute-done.5
  22.4 4.0 collective-permute-done.4
  37.2 3.8 collective-permute-done.2
  43.3 3.3 collective-permute-done.1
  54.9 8.6 collective-permute-done.11
  64.8 3.2 collective-permute-done.10
  74.0 3.6 collective-permute-start.8
  78.5 12.2 %collective-permute-done.8 = bf16[64,2048]{1,0:T(8,128)(2,1)S(1)} collective-permute-done((bf16[64,2048]{1,0:T(8,128)(2,1)S(1)}, bf16[64,2048]{1,0:T(8,128)(2,1)S(1)}, u32[]{:S(2)}, u32[]{:S(2)}) %collective-permute-start.8) | collective-permute-done | bytes 262176 | tf_op jit(solution)/shard_map/ppermute | solution.py:569
  90.6 10.5 %collective-permute-done.7 = bf16[64,2048]{1,0:T(8,128)(2,1)S(1)} collective-permute-done((bf16[64,2048]{1,0:T(8,128)(2,1)S(1)}, bf16[64,2048]{1,0:T(8,128)(2,1)S(1)}, u32[]{:S(2)}, u32[]{:S(2)}) %collective-permute-start.7) | collective-permute-done | bytes 262176 | tf_op jit(solution)/shard_map/ppermute | solution.py:569
  101.2 25.5 %collective-permute-done.6 = bf16[64,2048]{1,0:T(8,128)(2,1)S(1)} collective-permute-done((bf16[64,2048]{1,0:T(8,128)(2,1)S(1)}, bf16[64,2048]{1,0:T(8,128)(2,1)S(1)}, u32[]{:S(2)}, u32[]{:S(2)}) %collective-permute-start.6) | collective-permute-done | bytes 262176 | tf_op jit(solution)/shard_map/ppermute | solution.py:569
  129.9 22.4 %collective-permute-done.15.refs_1_ = bf16[4,64,2048]{2,1,0:T(8,128)(2,1)S(1)} collective-permute-done((bf16[4,64,2048]{2,1,0:T(8,128)(2,1)S(1)}, bf16[4,64,2048]{2,1,0:T(8,128)(2,1)S(1)}, u32[]{:S(2)}, u32[]{:S(2)}) %collective-permute-start.15) | collective-permute-done | bytes 1048608 | tf_op jit(solution)/shard_map/ppermute | solution.py:569
  161.7 8.5 collective-permute-done.18
  177.7 11.4 %shard_map.229.q_raw.k_raw.v_raw.refs_4_.refs_5_ = f32[1024,1536]{1,0:T(8,128)} custom-call(bf16[1024,2048]{1,0:T(8,128)(2,1)} %bitcast.385, bf16[8,4,64,2176]{3,2,1,0:T(8,128)(2,1)} %bitcast.415), custom_call_target="tpu_custom_call" | custom-call | flops 8589934592 | tf_op jit(solution)/shard_map/pallas_call | solution.py:183
  189.1 2.6 multiply_reduce_fusion.5
  201.8 6.1 collective-permute-done.19
  207.9 12.3 %collective-permute-done.20 = f32[2,1024]{0,1:T(8,128)} collective-permute-done((f32[2,1024]{0,1:T(8,128)}, f32[2,1024]{0,1:T(8,128)}, u32[]{:S(2)}, u32[]{:S(2)}) %collective-permute-start.20) | collective-permute-done | bytes 8224 | tf_op jit(solution)/shard_map/ppermute | solution.py:579
  222.7 15.8 %shard_map.230 = (bf16[1024,512]{1,0:T(8,128)(2,1)}, bf16[1024,512]{1,0:T(8,128)(2,1)}, bf16[1024,512]{1,0:T(8,128)(2,1)}, bf16[1024,512]{1,0:T(8,128)(2,1)}) custom-call(f32[1024,1536]{1,0:T(8,128)} %shard_map.229.q_raw.k_raw.v_raw.refs_4_.refs_5_, f32[1024,1536]{1,0:T(8,128)} %shard_map.229.q_raw.k_raw.v_raw.refs_4_.refs_5_, ...), custom_call_target="tpu_custom_call" | custom-call | tf_op jit(solution)/shard_map/pallas_call | solution.py:82
  238.4 5.9 shard_map.231
  247.2 12.6 %collective-permute-done.24 = bf16[2,64,2048]{2,1,0:T(8,128)(2,1)S(1)} collective-permute-done((bf16[2,64,2048]{2,1,0:T(8,128)(2,1)}, bf16[2,64,2048]{2,1,0:T(8,128)(2,1)S(1)}, u32[]{:S(2)}, u32[]{:S(2)}) %collective-permute-start.24) | collective-permute-done | bytes 524320 | tf_op jit(solution)/shard_map/ppermute | solution.py:569
  266.3 21.4 %collective-permute-done.27 = bf16[4,64,2048]{2,1,0:T(8,128)(2,1)S(1)} collective-permute-done((bf16[4,64,2048]{2,1,0:T(8,128)(2,1)}, bf16[4,64,2048]{2,1,0:T(8,128)(2,1)S(1)}, u32[]{:S(2)}, u32[]{:S(2)}) %collective-permute-start.27) | collective-permute-done | bytes 1048608 | tf_op jit(solution)/shard_map/ppermute | solution.py:569
  290.1 4.2 fusion.24
  296.6 21.1 %collective-permute-done.28.refs_1_ = bf16[4,64,2048]{2,1,0:T(8,128)(2,1)S(1)} collective-permute-done((bf16[4,64,2048]{2,1,0:T(8,128)(2,1)S(1)}, bf16[4,64,2048]{2,1,0:T(8,128)(2,1)S(1)}, u32[]{:S(2)}, u32[]{:S(2)}) %collective-permute-start.28) | collective-permute-done | bytes 1048608 | tf_op jit(solution)/shard_map/ppermute | solution.py:569
  326.3 7.2 collective-permute-done.31
  342.4 6.5 collective-permute-done.34.refs_5_
  348.9 4.3 collective-permute-done.33.refs_4_
  354.1 6.4 all-gather.7.cloned.1.call-done
  360.5 23.6 %shard_map.233 = (bf16[1024,2048]{1,0:T(8,128)(2,1)}, f32[1024,2048]{1,0:T(8,128)}, f32[1024,2048]{1,0:T(8,128)}) custom-call(bf16[1024,2048]{1,0:T(8,128)(2,1)} %bitcast.380, bf16[8,3,4,64,2048]{4,3,2,1,0:T(8,128)(2,1)} %bitcast.371, bf16[8,3,4,64,2048]{4,3,2,1,0:T(8,128)(2,1)} %bitcast.372, bf16[64,2048]{1,0:T(8,128)(2,1)} %copy-done.48, ...), custom_call_target="tpu_custom_call" | custom-call | flops 8589934592 | tf_op jit(solution)/shard_map/pallas_call | solution.py:183
  386.3 13.1 %shard_map.234 = (bf16[2,64,2048]{2,1,0:T(8,128)(2,1)}, bf16[2,64,2048]{2,1,0:T(8,128)(2,1)}, bf16[4,64,2048]{2,1,0:T(8,128)(2,1)}, bf16[4,64,2048]{2,1,0:T(8,128)(2,1)}, bf16[4,64,2048]{2,1,0:T(8,128)(2,1)}) custom-call(s32[2]{0:T(128)} %pad_add_fusion.refs_0_, bf16[1024,2048]{1,0:T(8,128)(2,1)} %get-tuple-element.555.refs_1_.a, ...), custom_call_target="tpu_custom_call" | custom-call | flops 8589934592 | tf_op jit(solution)/shard_map/pallas_call | solution.py:183
  404.0 3.2 collective-permute-start.40
  407.2 6.6 collective-permute-done.37
  419.8 6.8 collective-permute-done.40
  428.0 22.8 %collective-permute-done.39 = bf16[4,64,2048]{2,1,0:T(8,128)(2,1)S(1)} collective-permute-done((bf16[4,64,2048]{2,1,0:T(8,128)(2,1)S(1)}, bf16[4,64,2048]{2,1,0:T(8,128)(2,1)S(1)}, u32[]{:S(2)}, u32[]{:S(2)}) %collective-permute-start.39) | collective-permute-done | bytes 1048608 | tf_op jit(solution)/shard_map/ppermute | solution.py:569
  456.8 2.7 collective-permute-start.45
  461.2 6.8 collective-permute-done.45.refs_4_
  468.0 4.2 collective-permute-done.44.refs_3_
  472.2 6.5 collective-permute-done.43.refs_2_
  487.2 7.3 collective-permute-done.49
  497.9 18.2 %shard_map.236.refs_1_.refs_2_ = bf16[2,1024,2048]{2,1,0:T(8,128)(2,1)} custom-call(bf16[1024,2048]{1,0:T(8,128)(2,1)} %bitcast.387, bf16[8,3,4,64,2048]{4,3,2,1,0:T(8,128)(2,1)} %bitcast.374, f32[1024,2048]{1,0:T(8,128)} %get-tuple-element.549.refs_2_, f32[1024,2048]{1,0:T(8,128)} %get-tuple-element.550.refs_3_), custom_call_target="tpu_custom_call" | custom-call | flops 8589934592 | tf_op jit(solution)/shard_map/pallas_call | solution.py:183
  516.1 14.4 %shard_map.237 = bf16[4,1,256,2048]{3,2,1,0:T(8,128)(2,1)} custom-call(s32[1]{0:T(128)} %bitcast.116.core, bf16[1024,2048]{1,0:T(8,128)(2,1)} %get-tuple-element.555.refs_1_.a, bf16[1024,2048]{1,0:T(8,128)(2,1)} %bitcast.388, bf16[1024,2048]{1,0:T(8,128)(2,1)} %collective-permute-done.51.c, bf16[1024,2048]{1,0:T(8,128)(2,1)} %collective-permute-done.52.d), custom_call_target="tpu_custom_call" | custom-call | flops 8589934592 | tf_op jit(solution)/shard_map/pallas_call | solution.py:419
  530.6 26.2 %shard_map.238 = bf16[4,2,1,4,64,2048]{5,4,3,2,1,0:T(8,128)(2,1)} custom-call(bf16[1024,1024]{1,0:T(8,128)(2,1)} %pad_maximum_fusion.4.refs_0_, bf16[2,1024,2048]{2,1,0:T(8,128)(2,1)} %shard_map.236.refs_1_.refs_2_, bf16[1024,1024]{1,0:T(8,128)(2,1)} %collective-permute-done.35.refs_2_, bf16[2,1024,2048]{2,1,0:T(8,128)(2,1)} %collective-permute-done.50.refs_3_), custom_call_target="tpu_custom_call" | custom-call | flops 8589934592 | tf_op jit(solution)/shard_map/pallas_call | solution.py:183
  556.9 23.9 %shard_map.239 = (bf16[2,64,2048]{2,1,0:T(8,128)(2,1)}, bf16[2,64,2048]{2,1,0:T(8,128)(2,1)}, bf16[4,64,2048]{2,1,0:T(8,128)(2,1)}, bf16[4,64,2048]{2,1,0:T(8,128)(2,1)}, bf16[4,64,2048]{2,1,0:T(8,128)(2,1)}) custom-call(s32[2]{0:T(128)} %pad_add_fusion.refs_0_, bf16[2,1024,2048]{2,1,0:T(8,128)(2,1)} %shard_map.236.refs_1_.refs_2_, ...), custom_call_target="tpu_custom_call" | custom-call | flops 8589934592 | tf_op jit(solution)/shard_map/pallas_call | solution.py:183
  582.7 12.8 %collective-permute-done.54 = bf16[2,64,2048]{2,1,0:T(8,128)(2,1)S(1)} collective-permute-done((bf16[2,64,2048]{2,1,0:T(8,128)(2,1)}, bf16[2,64,2048]{2,1,0:T(8,128)(2,1)S(1)}, u32[]{:S(2)}, u32[]{:S(2)}) %collective-permute-start.54) | collective-permute-done | bytes 524320 | tf_op jit(solution)/shard_map/ppermute | solution.py:569
  601.8 21.4 %collective-permute-done.59 = bf16[4,64,2048]{2,1,0:T(8,128)(2,1)S(1)} collective-permute-done((bf16[4,64,2048]{2,1,0:T(8,128)(2,1)S(1)}, bf16[4,64,2048]{2,1,0:T(8,128)(2,1)S(1)}, u32[]{:S(2)}, u32[]{:S(2)}) %collective-permute-start.59) | collective-permute-done | bytes 1048608 | tf_op jit(solution)/shard_map/ppermute | solution.py:569
  632.5 20.3 %collective-permute-done.60.refs_1_ = bf16[4,64,2048]{2,1,0:T(8,128)(2,1)S(1)} collective-permute-done((bf16[4,64,2048]{2,1,0:T(8,128)(2,1)S(1)}, bf16[4,64,2048]{2,1,0:T(8,128)(2,1)S(1)}, u32[]{:S(2)}, u32[]{:S(2)}) %collective-permute-start.60) | collective-permute-done | bytes 1048608 | tf_op jit(solution)/shard_map/ppermute | solution.py:569
  652.8 6.5 collective-permute-done.61.refs_0_
  666.5 6.9 collective-permute-done.63
  675.6 6.3 shard_map.241.refs_3_
  682.8 22.8 %shard_map.242 = (f32[1024,512]{1,0:T(8,128)}, f32[1024,512]{1,0:T(8,128)}, bf16[1024,512]{1,0:T(8,128)(2,1)}, f32[1024,2]{1,0:T(8,128)}, f32[1,512]{1,0:T(1,128)}, /*index=5*/f32[1,512]{1,0:T(1,128)}) custom-call(bf16[1024,512]{1,0:T(8,128)(2,1)} %get-tuple-element.613.refs_0_, bf16[1024,512]{1,0:T(8,128)(2,1)} %get-tuple-element.614.refs_1_, ...), custom_call_target="tpu_custom_call" | custom-call | tf_op jit(solution)/shard_map/pallas_call | solution.py:165
  710.4 11.4 %collective-permute-done.64 = f32[2,1024]{0,1:T(8,128)S(1)} collective-permute-done((f32[2,1024]{0,1:T(8,128)S(1)}, f32[2,1024]{0,1:T(8,128)S(1)}, u32[]{:S(2)}, u32[]{:S(2)}) %collective-permute-start.64) | collective-permute-done | bytes 8224 | tf_op jit(solution)/shard_map/ppermute | solution.py:579
  721.7 6.6 collective-permute-done.65
  733.8 10.8 %shard_map.243 = (bf16[2,64,2048]{2,1,0:T(8,128)(2,1)}, bf16[2,64,2048]{2,1,0:T(8,128)(2,1)}, bf16[4,64,2048]{2,1,0:T(8,128)(2,1)}, bf16[4,64,2048]{2,1,0:T(8,128)(2,1)}, bf16[4,64,2048]{2,1,0:T(8,128)(2,1)}) custom-call(s32[2]{0:T(128)} %pad_add_fusion.refs_0_, bf16[1024,1536]{1,0:T(8,128)(2,1)} %copy-done.31, bf16[8,4,64,2176]{3,2,1,0:T(8,128)(2,1)} %bitcast.419), custom_call_target="tpu_custom_call" | custom-call | flops 8589934592 | tf_op jit(solution)/shard_map/pallas_call | solution.py:183
  746.8 5.8 reduce-scatter.6.cloned.1.call-done
  752.6 14.9 %shard_map.244 = bf16[4,1,4,64,2048]{4,3,2,1,0:T(8,128)(2,1)} custom-call(bf16[1024,1024]{1,0:T(8,128)(2,1)} %pad_maximum_fusion.2.refs_0_, bf16[1024,1536]{1,0:T(8,128)(2,1)} %copy-done.31, bf16[1024,1024]{1,0:T(8,128)(2,1)} %collective-permute-done.22.refs_2_, bf16[1024,1536]{1,0:T(8,128)(2,1)} %collective-permute-done.69.refs_3_, ...), custom_call_target="tpu_custom_call" | custom-call | flops 8589934592 | tf_op jit(solution)/shard_map/pallas_call | solution.py:183
  775.6 20.7 %collective-permute-done.72 = bf16[4,64,2048]{2,1,0:T(8,128)(2,1)} collective-permute-done((bf16[4,64,2048]{2,1,0:T(8,128)(2,1)}, bf16[4,64,2048]{2,1,0:T(8,128)(2,1)}, u32[]{:S(2)}, u32[]{:S(2)}) %collective-permute-start.72) | collective-permute-done | bytes 1048608 | tf_op jit(solution)/shard_map/ppermute | solution.py:569
  797.7 2.5 add_convert_fusion
  809.4 3.2 collective-permute-start.75
  816.0 3.8 collective-permute-done.82
  821.6 3.5 collective-permute-done.80
  825.1 3.5 collective-permute-start.73
  829.0 7.4 collective-permute-done.74
  836.4 26.7 %collective-permute-done.73 = bf16[64,2048]{1,0:T(8,128)(2,1)S(1)} collective-permute-done((bf16[64,2048]{1,0:T(8,128)(2,1)S(1)}, bf16[64,2048]{1,0:T(8,128)(2,1)S(1)}, u32[]{:S(2)}, u32[]{:S(2)}) %collective-permute-start.73) | collective-permute-done | bytes 262176 | tf_op jit(solution)/shard_map/ppermute | solution.py:569
  874.0 7.1 collective-permute-start.91
  890.0 2.8 collective-permute-done.89
  (555 shorter events, 219.8 us)
Async XLA Ops:
  7.2 170.5 %all-gather.5.cloned.1.call-start = ((), (), s32[]{:S(2)}) async-start(), calls=%async_computation.6 | async-start | bytes 10027008 | tf_op jit(solution)/shard_map/all_gather | solution.py:749
  30.7 329.8 %all-gather.7.cloned.1.call-start = ((), (), s32[]{:S(2)}) async-start(), calls=%async_computation.7 | async-start | bytes 28311552 | tf_op jit(solution)/shard_map/all_gather | solution.py:749
  33.7 14.4 %collective-permute-start = (bf16[64,2048]{1,0:T(8,128)(2,1)S(1)}, bf16[64,2048]{1,0:T(8,128)(2,1)}, u32[]{:S(2)}, u32[]{:S(2)}) collective-permute-start(bf16[64,2048]{1,0:T(8,128)(2,1)S(1)} %copy-done.82), channel_id=1, source_target_pairs={{0,16},{16,0},{1,17},{17,1},{2,18},{18,2},{3,19},{19,3},{4,20},{20... | collective-permute-start | bytes 786440 | tf_op jit(solution)/shard_map/ppermute | solution.py:569
  34.3 34.0 %collective-permute-start.14 = (bf16[64,2048]{1,0:T(8,128)(2,1)S(1)}, bf16[64,2048]{1,0:T(8,128)(2,1)}, u32[]{:S(2)}, u32[]{:S(2)}) collective-permute-start(bf16[64,2048]{1,0:T(8,128)(2,1)S(1)} %get-tuple-element.400), channel_id=1, source_target_pairs={{0,24},{8,16},{16,8},{24,0},{1,25},{9,17},{17,9},{25,1},{2,26},{10... | collective-permute-start | bytes 786440 | tf_op jit(solution)/shard_map/ppermute | solution.py:569
  36.7 31.7 %collective-permute-start.13 = (bf16[64,2048]{1,0:T(8,128)(2,1)S(1)}, bf16[64,2048]{1,0:T(8,128)(2,1)}, u32[]{:S(2)}, u32[]{:S(2)}) collective-permute-start(bf16[64,2048]{1,0:T(8,128)(2,1)S(1)} %get-tuple-element.399), channel_id=1, source_target_pairs={{0,8},{8,0},{1,9},{9,1},{2,10},{10,2},{3,11},{11,3},{4,12},{12,4},... | collective-permute-start | bytes 786440 | tf_op jit(solution)/shard_map/ppermute | solution.py:569
  41.0 22.5 %collective-permute-start.11 = (bf16[64,2048]{1,0:T(8,128)(2,1)S(1)}, bf16[64,2048]{1,0:T(8,128)(2,1)S(1)}, u32[]{:S(2)}, u32[]{:S(2)}) collective-permute-start(bf16[64,2048]{1,0:T(8,128)(2,1)S(1)} %copy-done.81), channel_id=1, source_target_pairs={{0,24},{8,16},{16,8},{24,0},{1,25},{9,17},{17,9},{25,1},{2,26},{10... | collective-permute-start | bytes 786440 | tf_op jit(solution)/shard_map/ppermute | solution.py:569
  46.6 21.4 %collective-permute-start.10 = (bf16[64,2048]{1,0:T(8,128)(2,1)S(1)}, bf16[64,2048]{1,0:T(8,128)(2,1)S(1)}, u32[]{:S(2)}, u32[]{:S(2)}) collective-permute-start(bf16[64,2048]{1,0:T(8,128)(2,1)S(1)} %copy-done.80), channel_id=1, source_target_pairs={{0,8},{8,0},{1,9},{9,1},{2,10},{10,2},{3,11},{11,3},{4,12},{12,4},... | collective-permute-start | bytes 786440 | tf_op jit(solution)/shard_map/ppermute | solution.py:569
  48.1 19.9 %collective-permute-start.9 = (bf16[64,2048]{1,0:T(8,128)(2,1)S(1)}, bf16[64,2048]{1,0:T(8,128)(2,1)S(1)}, u32[]{:S(2)}, u32[]{:S(2)}) collective-permute-start(bf16[64,2048]{1,0:T(8,128)(2,1)S(1)} %copy-done.79), channel_id=1, source_target_pairs={{0,16},{16,0},{1,17},{17,1},{2,18},{18,2},{3,19},{19,3},{4,20},{20... | collective-permute-start | bytes 786440 | tf_op jit(solution)/shard_map/ppermute | solution.py:569
  74.0 608.0 %reduce-scatter.4.cloned.1.call-start = ((), (), s32[]{:S(2)}) async-start(), calls=%async_computation.3 | async-start | bytes 5242880 | tf_op jit(solution)/shard_map/reduce_scatter | solution.py:754
  74.0 16.6 %collective-permute-start.8 = (bf16[64,2048]{1,0:T(8,128)(2,1)S(1)}, bf16[64,2048]{1,0:T(8,128)(2,1)S(1)}, u32[]{:S(2)}, u32[]{:S(2)}) collective-permute-start(bf16[64,2048]{1,0:T(8,128)(2,1)S(1)} %get-tuple-element.389), channel_id=1, source_target_pairs={{0,3},{1,2},{2,1},{3,0},{4,7},{5,6},{6,5},{7,4},{8,11},{9,10},{10,... | collective-permute-start | bytes 786440 | tf_op jit(solution)/shard_map/ppermute | solution.py:569
  77.6 23.5 %collective-permute-start.7 = (bf16[64,2048]{1,0:T(8,128)(2,1)S(1)}, bf16[64,2048]{1,0:T(8,128)(2,1)S(1)}, u32[]{:S(2)}, u32[]{:S(2)}) collective-permute-start(bf16[64,2048]{1,0:T(8,128)(2,1)S(1)} %get-tuple-element.388), channel_id=1, source_target_pairs={{0,1},{1,0},{2,3},{3,2},{4,5},{5,4},{6,7},{7,6},{8,9},{9,8},{10,11... | collective-permute-start | bytes 786440 | tf_op jit(solution)/shard_map/ppermute | solution.py:569
  77.6 49.0 %collective-permute-start.6 = (bf16[64,2048]{1,0:T(8,128)(2,1)S(1)}, bf16[64,2048]{1,0:T(8,128)(2,1)S(1)}, u32[]{:S(2)}, u32[]{:S(2)}) collective-permute-start(bf16[64,2048]{1,0:T(8,128)(2,1)S(1)} %get-tuple-element.387), channel_id=1, source_target_pairs={{0,2},{2,0},{1,3},{3,1},{4,6},{6,4},{5,7},{7,5},{8,10},{10,8},{9,1... | collective-permute-start | bytes 786440 | tf_op jit(solution)/shard_map/ppermute | solution.py:569
  126.9 25.4 %collective-permute-start.15 = (bf16[4,64,2048]{2,1,0:T(8,128)(2,1)S(1)}, bf16[4,64,2048]{2,1,0:T(8,128)(2,1)S(1)}, u32[]{:S(2)}, u32[]{:S(2)}) collective-permute-start(bf16[4,64,2048]{2,1,0:T(8,128)(2,1)S(1)} %bitcast.389), channel_id=1, source_target_pairs={{0,8},{8,0},{1,9},{9,1},{2,10},{10,2},{3,11},{11,3},{4,12},{12,4},... | collective-permute-start | bytes 3145736 | tf_op jit(solution)/shard_map/ppermute | solution.py:569
  128.5 25.0 %collective-permute-start.16 = (bf16[4,64,2048]{2,1,0:T(8,128)(2,1)S(1)}, bf16[4,64,2048]{2,1,0:T(8,128)(2,1)S(1)}, u32[]{:S(2)}, u32[]{:S(2)}) collective-permute-start(bf16[4,64,2048]{2,1,0:T(8,128)(2,1)S(1)} %bitcast.390), channel_id=1, source_target_pairs={{0,16},{16,0},{1,17},{17,1},{2,18},{18,2},{3,19},{19,3},{4,20},{20... | collective-permute-start | bytes 3145736 | tf_op jit(solution)/shard_map/ppermute | solution.py:569
  175.0 21.3 %collective-permute-start.22 = (bf16[1024,1024]{1,0:T(8,128)(2,1)S(1)}, bf16[1024,1024]{1,0:T(8,128)(2,1)}, u32[]{:S(2)}, u32[]{:S(2)}) collective-permute-start(bf16[1024,1024]{1,0:T(8,128)(2,1)S(1)} %pad_maximum_fusion.3), channel_id=1, source_target_pairs={{0,4},{4,0},{1,5},{5,1},{2,6},{6,2},{3,7},{7,3},{8,12},{12,8},{9,1... | collective-permute-start | bytes 6291464 | tf_op jit(solution)/shard_map/ppermute | solution.py:569
  192.8 15.1 %collective-permute-start.19 = (f32[2,1024]{0,1:T(8,128)}, f32[2,1024]{0,1:T(8,128)}, u32[]{:S(2)}, u32[]{:S(2)}) collective-permute-start(f32[2,1024]{0,1:T(8,128)} %copy.92), channel_id=1, source_target_pairs={{0,8},{8,0},{1,9},{9,1},{2,10},{10,2},{3,11},{11,3},{4,12},{12,4},... | collective-permute-start | bytes 24584 | tf_op jit(solution)/shard_map/ppermute | solution.py:579
  194.3 25.9 %collective-permute-start.20 = (f32[2,1024]{0,1:T(8,128)}, f32[2,1024]{0,1:T(8,128)}, u32[]{:S(2)}, u32[]{:S(2)}) collective-permute-start(f32[2,1024]{0,1:T(8,128)} %copy.92), channel_id=1, source_target_pairs={{0,16},{16,0},{1,17},{17,1},{2,18},{18,2},{3,19},{19,3},{4,20},{20... | collective-permute-start | bytes 24584 | tf_op jit(solution)/shard_map/ppermute | solution.py:579
  195.3 24.9 %collective-permute-start.21 = (f32[2,1024]{0,1:T(8,128)}, f32[2,1024]{0,1:T(8,128)}, u32[]{:S(2)}, u32[]{:S(2)}) collective-permute-start(f32[2,1024]{0,1:T(8,128)} %copy.92), channel_id=1, source_target_pairs={{0,24},{8,16},{16,8},{24,0},{1,25},{9,17},{17,9},{25,1},{2,26},{10... | collective-permute-start | bytes 24584 | tf_op jit(solution)/shard_map/ppermute | solution.py:743
  245.2 14.5 %collective-permute-start.24 = (bf16[2,64,2048]{2,1,0:T(8,128)(2,1)}, bf16[2,64,2048]{2,1,0:T(8,128)(2,1)S(1)}, u32[]{:S(2)}, u32[]{:S(2)}) collective-permute-start(bf16[2,64,2048]{2,1,0:T(8,128)(2,1)} %get-tuple-element.453), channel_id=1, source_target_pairs={{0,16},{16,0},{1,17},{17,1},{2,18},{18,2},{3,19},{19,3},{4,20},{20... | collective-permute-start | bytes 1572872 | tf_op jit(solution)/shard_map/ppermute | solution.py:569
  262.9 24.8 %collective-permute-start.27 = (bf16[4,64,2048]{2,1,0:T(8,128)(2,1)}, bf16[4,64,2048]{2,1,0:T(8,128)(2,1)S(1)}, u32[]{:S(2)}, u32[]{:S(2)}) collective-permute-start(bf16[4,64,2048]{2,1,0:T(8,128)(2,1)} %pad_maximum_fusion.8), channel_id=1, source_target_pairs={{0,8},{8,0},{1,9},{9,1},{2,10},{10,2},{3,11},{11,3},{4,12},{12,4},... | collective-permute-start | bytes 3145736 | tf_op jit(solution)/shard_map/ppermute | solution.py:569
  263.7 24.6 %collective-permute-start.26 = (bf16[4,64,2048]{2,1,0:T(8,128)(2,1)}, bf16[4,64,2048]{2,1,0:T(8,128)(2,1)}, u32[]{:S(2)}, u32[]{:S(2)}) collective-permute-start(bf16[4,64,2048]{2,1,0:T(8,128)(2,1)} %pad_maximum_fusion.7), channel_id=1, source_target_pairs={{0,16},{16,0},{1,17},{17,1},{2,18},{18,2},{3,19},{19,3},{4,20},{20... | collective-permute-start | bytes 3145736 | tf_op jit(solution)/shard_map/ppermute | solution.py:569
  294.3 23.5 %collective-permute-start.28 = (bf16[4,64,2048]{2,1,0:T(8,128)(2,1)S(1)}, bf16[4,64,2048]{2,1,0:T(8,128)(2,1)S(1)}, u32[]{:S(2)}, u32[]{:S(2)}) collective-permute-start(bf16[4,64,2048]{2,1,0:T(8,128)(2,1)S(1)} %get-tuple-element.472), channel_id=1, source_target_pairs={{0,8},{8,0},{1,9},{9,1},{2,10},{10,2},{3,11},{11,3},{4,12},{12,4},... | collective-permute-start | bytes 3145736 | tf_op jit(solution)/shard_map/ppermute | solution.py:569
  295.4 23.1 %collective-permute-start.29 = (bf16[4,64,2048]{2,1,0:T(8,128)(2,1)S(1)}, bf16[4,64,2048]{2,1,0:T(8,128)(2,1)S(1)}, u32[]{:S(2)}, u32[]{:S(2)}) collective-permute-start(bf16[4,64,2048]{2,1,0:T(8,128)(2,1)S(1)} %get-tuple-element.472), channel_id=1, source_target_pairs={{0,16},{16,0},{1,17},{17,1},{2,18},{18,2},{3,19},{19,3},{4,20},{20... | collective-permute-start | bytes 3145736 | tf_op jit(solution)/shard_map/ppermute | solution.py:569
  338.9 15.2 %collective-permute-start.35 = (bf16[1024,1024]{1,0:T(8,128)(2,1)S(1)}, bf16[1024,1024]{1,0:T(8,128)(2,1)}, u32[]{:S(2)}, u32[]{:S(2)}) collective-permute-start(bf16[1024,1024]{1,0:T(8,128)(2,1)S(1)} %pad_maximum_fusion.5), channel_id=1, source_target_pairs={{0,4},{4,0},{1,5},{5,1},{2,6},{6,2},{3,7},{7,3},{8,12},{12,8},{9,1... | collective-permute-start | bytes 6291464 | tf_op jit(solution)/shard_map/ppermute | solution.py:569
  399.4 14.4 %collective-permute-start.37 = (bf16[2,64,2048]{2,1,0:T(8,128)(2,1)}, bf16[2,64,2048]{2,1,0:T(8,128)(2,1)}, u32[]{:S(2)}, u32[]{:S(2)}) collective-permute-start(bf16[2,64,2048]{2,1,0:T(8,128)(2,1)} %get-tuple-element.507), channel_id=1, source_target_pairs={{0,16},{16,0},{1,17},{17,1},{2,18},{18,2},{3,19},{19,3},{4,20},{20... | collective-permute-start | bytes 1572872 | tf_op jit(solution)/shard_map/ppermute | solution.py:569
  402.8 16.1 %collective-permute-start.42 = (bf16[64,2048]{1,0:T(8,128)(2,1)}, bf16[64,2048]{1,0:T(8,128)(2,1)S(1)}, u32[]{:S(2)}, u32[]{:S(2)}) collective-permute-start(bf16[64,2048]{1,0:T(8,128)(2,1)} %get-tuple-element.516), channel_id=1, source_target_pairs={{0,3},{1,2},{2,1},{3,0},{4,7},{5,6},{6,5},{7,4},{8,11},{9,10},{10,... | collective-permute-start | bytes 786440 | tf_op jit(solution)/shard_map/ppermute | solution.py:569
  403.3 16.5 %collective-permute-start.41 = (bf16[64,2048]{1,0:T(8,128)(2,1)}, bf16[64,2048]{1,0:T(8,128)(2,1)S(1)}, u32[]{:S(2)}, u32[]{:S(2)}) collective-permute-start(bf16[64,2048]{1,0:T(8,128)(2,1)} %get-tuple-element.515), channel_id=1, source_target_pairs={{0,1},{1,0},{2,3},{3,2},{4,5},{5,4},{6,7},{7,6},{8,9},{9,8},{10,11... | collective-permute-start | bytes 786440 | tf_op jit(solution)/shard_map/ppermute | solution.py:569
  404.0 22.7 %collective-permute-start.40 = (bf16[64,2048]{1,0:T(8,128)(2,1)}, bf16[64,2048]{1,0:T(8,128)(2,1)S(1)}, u32[]{:S(2)}, u32[]{:S(2)}) collective-permute-start(bf16[64,2048]{1,0:T(8,128)(2,1)} %get-tuple-element.514), channel_id=1, source_target_pairs={{0,2},{2,0},{1,3},{3,1},{4,6},{6,4},{5,7},{7,5},{8,10},{10,8},{9,1... | collective-permute-start | bytes 786440 | tf_op jit(solution)/shard_map/ppermute | solution.py:569
  426.6 24.2 %collective-permute-start.39 = (bf16[4,64,2048]{2,1,0:T(8,128)(2,1)S(1)}, bf16[4,64,2048]{2,1,0:T(8,128)(2,1)S(1)}, u32[]{:S(2)}, u32[]{:S(2)}) collective-permute-start(bf16[4,64,2048]{2,1,0:T(8,128)(2,1)S(1)} %pad_maximum_fusion.10), channel_id=1, source_target_pairs={{0,8},{8,0},{1,9},{9,1},{2,10},{10,2},{3,11},{11,3},{4,12},{12,4},... | collective-permute-start | bytes 3145736 | tf_op jit(solution)/shard_map/ppermute | solution.py:569
  427.2 23.9 %collective-permute-start.38 = (bf16[4,64,2048]{2,1,0:T(8,128)(2,1)S(1)}, bf16[4,64,2048]{2,1,0:T(8,128)(2,1)S(1)}, u32[]{:S(2)}, u32[]{:S(2)}) collective-permute-start(bf16[4,64,2048]{2,1,0:T(8,128)(2,1)S(1)} %pad_maximum_fusion.9), channel_id=1, source_target_pairs={{0,16},{16,0},{1,17},{17,1},{2,18},{18,2},{3,19},{19,3},{4,20},{20... | collective-permute-start | bytes 3145736 | tf_op jit(solution)/shard_map/ppermute | solution.py:569
  454.6 24.1 %collective-permute-start.46 = (bf16[4,64,2048]{2,1,0:T(8,128)(2,1)S(1)}, bf16[4,64,2048]{2,1,0:T(8,128)(2,1)S(1)}, u32[]{:S(2)}, u32[]{:S(2)}) collective-permute-start(bf16[4,64,2048]{2,1,0:T(8,128)(2,1)S(1)} %get-tuple-element.539), channel_id=1, source_target_pairs={{0,8},{8,0},{1,9},{9,1},{2,10},{10,2},{3,11},{11,3},{4,12},{12,4},... | collective-permute-start | bytes 3145736 | tf_op jit(solution)/shard_map/ppermute | solution.py:569
  456.2 22.7 %collective-permute-start.47 = (bf16[4,64,2048]{2,1,0:T(8,128)(2,1)S(1)}, bf16[4,64,2048]{2,1,0:T(8,128)(2,1)S(1)}, u32[]{:S(2)}, u32[]{:S(2)}) collective-permute-start(bf16[4,64,2048]{2,1,0:T(8,128)(2,1)S(1)} %get-tuple-element.539), channel_id=1, source_target_pairs={{0,16},{16,0},{1,17},{17,1},{2,18},{18,2},{3,19},{19,3},{4,20},{20... | collective-permute-start | bytes 3145736 | tf_op jit(solution)/shard_map/ppermute | solution.py:569
  459.5 19.2 %collective-permute-start.43 = (bf16[64,2048]{1,0:T(8,128)(2,1)S(1)}, bf16[64,2048]{1,0:T(8,128)(2,1)S(1)}, u32[]{:S(2)}, u32[]{:S(2)}) collective-permute-start(bf16[64,2048]{1,0:T(8,128)(2,1)S(1)} %get-tuple-element.528), channel_id=1, source_target_pairs={{0,2},{2,0},{1,3},{3,1},{4,6},{6,4},{5,7},{7,5},{8,10},{10,8},{9,1... | collective-permute-start | bytes 786440 | tf_op jit(solution)/shard_map/ppermute | solution.py:569
  468.0 48.1 %collective-permute-start.51 = (bf16[1024,2048]{1,0:T(8,128)(2,1)}, bf16[1024,2048]{1,0:T(8,128)(2,1)}, u32[]{:S(2)}, u32[]{:S(2)}) collective-permute-start(bf16[1024,2048]{1,0:T(8,128)(2,1)} %get-tuple-element.555.refs_1_.a), channel_id=1, source_target_pairs={{0,4},{4,0},{1,5},{5,1},{2,6},{6,2},{3,7},{7,3},{8,12},{12,8},{9,1... | collective-permute-start | bytes 12582920 | tf_op jit(solution)/shard_map/ppermute | solution.py:569
  495.9 20.2 %collective-permute-start.52 = (bf16[1024,2048]{1,0:T(8,128)(2,1)S(1)}, bf16[1024,2048]{1,0:T(8,128)(2,1)}, u32[]{:S(2)}, u32[]{:S(2)}) collective-permute-start(bf16[1024,2048]{1,0:T(8,128)(2,1)S(1)} %bitcast.386), channel_id=1, source_target_pairs={{0,4},{4,0},{1,5},{5,1},{2,6},{6,2},{3,7},{7,3},{8,12},{12,8},{9,1... | collective-permute-start | bytes 12582920 | tf_op jit(solution)/shard_map/ppermute | solution.py:569
  516.1 14.4 %collective-permute-start.50 = (bf16[2,1024,2048]{2,1,0:T(8,128)(2,1)}, bf16[2,1024,2048]{2,1,0:T(8,128)(2,1)}, u32[]{:S(2)}, u32[]{:S(2)}) collective-permute-start(bf16[2,1024,2048]{2,1,0:T(8,128)(2,1)} %shard_map.236.refs_1_.refs_2_), channel_id=1, source_target_pairs={{0,4},{4,0},{1,5},{5,1},{2,6},{6,2},{3,7},{7,3},{8,12},{12,8},{9,1... | collective-permute-start | bytes 25165832 | tf_op jit(solution)/shard_map/ppermute | solution.py:569
  530.5 222.1 %reduce-scatter.6.cloned.1.call-start = ((), (), s32[]{:S(2)}) async-start(), calls=%async_computation.4 | async-start | bytes 10485760 | tf_op jit(solution)/shard_map/reduce_scatter | solution.py:754
  556.8 312.4 %reduce-scatter.8.cloned.1.call-start = ((), (), s32[]{:S(2)}) async-start(), calls=%async_computation.5 | async-start | bytes 5242880 | tf_op jit(solution)/shard_map/reduce_scatter | solution.py:754
  580.8 14.6 %collective-permute-start.54 = (bf16[2,64,2048]{2,1,0:T(8,128)(2,1)}, bf16[2,64,2048]{2,1,0:T(8,128)(2,1)S(1)}, u32[]{:S(2)}, u32[]{:S(2)}) collective-permute-start(bf16[2,64,2048]{2,1,0:T(8,128)(2,1)} %get-tuple-element.572), channel_id=1, source_target_pairs={{0,16},{16,0},{1,17},{17,1},{2,18},{18,2},{3,19},{19,3},{4,20},{20... | collective-permute-start | bytes 1572872 | tf_op jit(solution)/shard_map/ppermute | solution.py:569
  581.3 14.3 %collective-permute-start.53 = (bf16[2,64,2048]{2,1,0:T(8,128)(2,1)}, bf16[2,64,2048]{2,1,0:T(8,128)(2,1)S(1)}, u32[]{:S(2)}, u32[]{:S(2)}) collective-permute-start(bf16[2,64,2048]{2,1,0:T(8,128)(2,1)} %get-tuple-element.571), channel_id=1, source_target_pairs={{0,8},{8,0},{1,9},{9,1},{2,10},{10,2},{3,11},{11,3},{4,12},{12,4},... | collective-permute-start | bytes 1572872 | tf_op jit(solution)/shard_map/ppermute | solution.py:569
  598.4 24.8 %collective-permute-start.59 = (bf16[4,64,2048]{2,1,0:T(8,128)(2,1)S(1)}, bf16[4,64,2048]{2,1,0:T(8,128)(2,1)S(1)}, u32[]{:S(2)}, u32[]{:S(2)}) collective-permute-start(bf16[4,64,2048]{2,1,0:T(8,128)(2,1)S(1)} %pad_maximum_fusion.12), channel_id=1, source_target_pairs={{0,8},{8,0},{1,9},{9,1},{2,10},{10,2},{3,11},{11,3},{4,12},{12,4},... | collective-permute-start | bytes 3145736 | tf_op jit(solution)/shard_map/ppermute | solution.py:569
  599.8 24.3 %collective-permute-start.58 = (bf16[4,64,2048]{2,1,0:T(8,128)(2,1)S(1)}, bf16[4,64,2048]{2,1,0:T(8,128)(2,1)S(1)}, u32[]{:S(2)}, u32[]{:S(2)}) collective-permute-start(bf16[4,64,2048]{2,1,0:T(8,128)(2,1)S(1)} %pad_maximum_fusion.11), channel_id=1, source_target_pairs={{0,16},{16,0},{1,17},{17,1},{2,18},{18,2},{3,19},{19,3},{4,20},{20... | collective-permute-start | bytes 3145736 | tf_op jit(solution)/shard_map/ppermute | solution.py:569
  626.7 26.1 %collective-permute-start.60 = (bf16[4,64,2048]{2,1,0:T(8,128)(2,1)S(1)}, bf16[4,64,2048]{2,1,0:T(8,128)(2,1)S(1)}, u32[]{:S(2)}, u32[]{:S(2)}) collective-permute-start(bf16[4,64,2048]{2,1,0:T(8,128)(2,1)S(1)} %multiply_convert_fusion.2), channel_id=1, source_target_pairs={{0,8},{8,0},{1,9},{9,1},{2,10},{10,2},{3,11},{11,3},{4,12},{12,4},... | collective-permute-start | bytes 3145736 | tf_op jit(solution)/shard_map/ppermute | solution.py:569
  627.5 31.7 %collective-permute-start.61 = (bf16[4,64,2048]{2,1,0:T(8,128)(2,1)S(1)}, bf16[4,64,2048]{2,1,0:T(8,128)(2,1)S(1)}, u32[]{:S(2)}, u32[]{:S(2)}) collective-permute-start(bf16[4,64,2048]{2,1,0:T(8,128)(2,1)S(1)} %multiply_convert_fusion.2), channel_id=1, source_target_pairs={{0,16},{16,0},{1,17},{17,1},{2,18},{18,2},{3,19},{19,3},{4,20},{20... | collective-permute-start | bytes 3145736 | tf_op jit(solution)/shard_map/ppermute | solution.py:569
  629.0 53.0 %collective-permute-start.57 = (bf16[64,2048]{1,0:T(8,128)(2,1)}, bf16[64,2048]{1,0:T(8,128)(2,1)S(1)}, u32[]{:S(2)}, u32[]{:S(2)}) collective-permute-start(bf16[64,2048]{1,0:T(8,128)(2,1)} %get-tuple-element.583), channel_id=1, source_target_pairs={{0,24},{8,16},{16,8},{24,0},{1,25},{9,17},{17,9},{25,1},{2,26},{10... | collective-permute-start | bytes 786440 | tf_op jit(solution)/shard_map/ppermute | solution.py:569
  630.2 51.8 %collective-permute-start.56 = (bf16[64,2048]{1,0:T(8,128)(2,1)}, bf16[64,2048]{1,0:T(8,128)(2,1)S(1)}, u32[]{:S(2)}, u32[]{:S(2)}) collective-permute-start(bf16[64,2048]{1,0:T(8,128)(2,1)} %get-tuple-element.582), channel_id=1, source_target_pairs={{0,8},{8,0},{1,9},{9,1},{2,10},{10,2},{3,11},{11,3},{4,12},{12,4},... | collective-permute-start | bytes 786440 | tf_op jit(solution)/shard_map/ppermute | solution.py:569
  631.0 50.9 %collective-permute-start.55 = (bf16[64,2048]{1,0:T(8,128)(2,1)}, bf16[64,2048]{1,0:T(8,128)(2,1)S(1)}, u32[]{:S(2)}, u32[]{:S(2)}) collective-permute-start(bf16[64,2048]{1,0:T(8,128)(2,1)} %get-tuple-element.581), channel_id=1, source_target_pairs={{0,16},{16,0},{1,17},{17,1},{2,18},{18,2},{3,19},{19,3},{4,20},{20... | collective-permute-start | bytes 786440 | tf_op jit(solution)/shard_map/ppermute | solution.py:569
  706.8 14.9 %collective-permute-start.64 = (f32[2,1024]{0,1:T(8,128)S(1)}, f32[2,1024]{0,1:T(8,128)S(1)}, u32[]{:S(2)}, u32[]{:S(2)}) collective-permute-start(f32[2,1024]{0,1:T(8,128)S(1)} %multiply_bitcast_fusion), channel_id=1, source_target_pairs={{0,8},{8,0},{1,9},{9,1},{2,10},{10,2},{3,11},{11,3},{4,12},{12,4},... | collective-permute-start | bytes 24584 | tf_op jit(solution)/shard_map/ppermute | solution.py:579
  707.8 20.5 %collective-permute-start.65 = (f32[2,1024]{0,1:T(8,128)S(1)}, f32[2,1024]{0,1:T(8,128)S(1)}, u32[]{:S(2)}, u32[]{:S(2)}) collective-permute-start(f32[2,1024]{0,1:T(8,128)S(1)} %multiply_bitcast_fusion), channel_id=1, source_target_pairs={{0,16},{16,0},{1,17},{17,1},{2,18},{18,2},{3,19},{19,3},{4,20},{20... | collective-permute-start | bytes 24584 | tf_op jit(solution)/shard_map/ppermute | solution.py:579
  708.2 20.1 %collective-permute-start.66 = (f32[2,1024]{0,1:T(8,128)S(1)}, f32[2,1024]{0,1:T(8,128)S(1)}, u32[]{:S(2)}, u32[]{:S(2)}) collective-permute-start(f32[2,1024]{0,1:T(8,128)S(1)} %multiply_bitcast_fusion), channel_id=1, source_target_pairs={{0,24},{8,16},{16,8},{24,0},{1,25},{9,17},{17,9},{25,1},{2,26},{10... | collective-permute-start | bytes 24584 | tf_op jit(solution)/shard_map/ppermute | solution.py:743
  710.4 36.4 %collective-permute-start.70 = (bf16[1024,2048]{1,0:T(8,128)(2,1)}, bf16[1024,2048]{1,0:T(8,128)(2,1)}, u32[]{:S(2)}, u32[]{:S(2)}) collective-permute-start(bf16[1024,2048]{1,0:T(8,128)(2,1)} %bitcast.398), channel_id=1, source_target_pairs={{0,4},{4,0},{1,5},{5,1},{2,6},{6,2},{3,7},{7,3},{8,12},{12,8},{9,1... | collective-permute-start | bytes 12582920 | tf_op jit(solution)/shard_map/ppermute | solution.py:579
  732.1 14.7 %collective-permute-start.69 = (bf16[1024,1536]{1,0:T(8,128)(2,1)S(1)}, bf16[1024,1536]{1,0:T(8,128)(2,1)}, u32[]{:S(2)}, u32[]{:S(2)}) collective-permute-start(bf16[1024,1536]{1,0:T(8,128)(2,1)S(1)} %pad_maximum_fusion.1.refs_1_), channel_id=1, source_target_pairs={{0,4},{4,0},{1,5},{5,1},{2,6},{6,2},{3,7},{7,3},{8,12},{12,8},{9,1... | collective-permute-start | bytes 9437192 | tf_op jit(solution)/shard_map/ppermute | solution.py:579
  744.6 22.8 %collective-permute-start.68 = (bf16[2,64,2048]{2,1,0:T(8,128)(2,1)}, bf16[2,64,2048]{2,1,0:T(8,128)(2,1)}, u32[]{:S(2)}, u32[]{:S(2)}) collective-permute-start(bf16[2,64,2048]{2,1,0:T(8,128)(2,1)} %get-tuple-element.649), channel_id=1, source_target_pairs={{0,16},{16,0},{1,17},{17,1},{2,18},{18,2},{3,19},{19,3},{4,20},{20... | collective-permute-start | bytes 1572872 | tf_op jit(solution)/shard_map/ppermute | solution.py:569
  745.5 21.9 %collective-permute-start.67 = (bf16[2,64,2048]{2,1,0:T(8,128)(2,1)}, bf16[2,64,2048]{2,1,0:T(8,128)(2,1)}, u32[]{:S(2)}, u32[]{:S(2)}) collective-permute-start(bf16[2,64,2048]{2,1,0:T(8,128)(2,1)} %get-tuple-element.648), channel_id=1, source_target_pairs={{0,8},{8,0},{1,9},{9,1},{2,10},{10,2},{3,11},{11,3},{4,12},{12,4},... | collective-permute-start | bytes 1572872 | tf_op jit(solution)/shard_map/ppermute | solution.py:569
  771.2 25.1 %collective-permute-start.72 = (bf16[4,64,2048]{2,1,0:T(8,128)(2,1)}, bf16[4,64,2048]{2,1,0:T(8,128)(2,1)}, u32[]{:S(2)}, u32[]{:S(2)}) collective-permute-start(bf16[4,64,2048]{2,1,0:T(8,128)(2,1)} %pad_maximum_fusion.14), channel_id=1, source_target_pairs={{0,8},{8,0},{1,9},{9,1},{2,10},{10,2},{3,11},{11,3},{4,12},{12,4},... | collective-permute-start | bytes 3145736 | tf_op jit(solution)/shard_map/ppermute | solution.py:569
  772.7 24.9 %collective-permute-start.71 = (bf16[4,64,2048]{2,1,0:T(8,128)(2,1)S(1)}, bf16[4,64,2048]{2,1,0:T(8,128)(2,1)}, u32[]{:S(2)}, u32[]{:S(2)}) collective-permute-start(bf16[4,64,2048]{2,1,0:T(8,128)(2,1)S(1)} %pad_maximum_fusion.13), channel_id=1, source_target_pairs={{0,16},{16,0},{1,17},{17,1},{2,18},{18,2},{3,19},{19,3},{4,20},{20... | collective-permute-start | bytes 3145736 | tf_op jit(solution)/shard_map/ppermute | solution.py:569
  775.0 25.3 %collective-permute-start.76 = (f32[4,2,2,2,2,64]{5,4,3,0,2,1:T(2,128)S(1)}, f32[4,2,2,2,2,64]{5,4,3,0,2,1:T(2,128)S(1)}, u32[]{:S(2)}, u32[]{:S(2)}) collective-permute-start(f32[4,2,2,2,2,64]{5,4,3,0,2,1:T(2,128)S(1)} %get-tuple-element.675), channel_id=1, source_target_pairs={{0,16},{16,0},{1,17},{17,1},{2,18},{18,2},{3,19},{19,3},{4,20},{20... | collective-permute-start | bytes 49160 | tf_op jit(solution)/shard_map/ppermute | solution.py:569
  809.4 19.6 %collective-permute-start.75 = (bf16[64,2048]{1,0:T(8,128)(2,1)S(1)}, bf16[64,2048]{1,0:T(8,128)(2,1)S(1)}, u32[]{:S(2)}, u32[]{:S(2)}) collective-permute-start(bf16[64,2048]{1,0:T(8,128)(2,1)S(1)} %get-tuple-element.674), channel_id=1, source_target_pairs={{0,3},{1,2},{2,1},{3,0},{4,7},{5,6},{6,5},{7,4},{8,11},{9,10},{10,... | collective-permute-start | bytes 786440 | tf_op jit(solution)/shard_map/ppermute | solution.py:569
  812.7 23.7 %collective-permute-start.74 = (bf16[64,2048]{1,0:T(8,128)(2,1)S(1)}, bf16[64,2048]{1,0:T(8,128)(2,1)S(1)}, u32[]{:S(2)}, u32[]{:S(2)}) collective-permute-start(bf16[64,2048]{1,0:T(8,128)(2,1)S(1)} %get-tuple-element.673), channel_id=1, source_target_pairs={{0,1},{1,0},{2,3},{3,2},{4,5},{5,4},{6,7},{7,6},{8,9},{9,8},{10,11... | collective-permute-start | bytes 786440 | tf_op jit(solution)/shard_map/ppermute | solution.py:569
  825.1 38.0 %collective-permute-start.73 = (bf16[64,2048]{1,0:T(8,128)(2,1)S(1)}, bf16[64,2048]{1,0:T(8,128)(2,1)S(1)}, u32[]{:S(2)}, u32[]{:S(2)}) collective-permute-start(bf16[64,2048]{1,0:T(8,128)(2,1)S(1)} %get-tuple-element.672), channel_id=1, source_target_pairs={{0,2},{2,0},{1,3},{3,1},{4,6},{6,4},{5,7},{7,5},{8,10},{10,8},{9,1... | collective-permute-start | bytes 786440 | tf_op jit(solution)/shard_map/ppermute | solution.py:569
  828.6 42.7 %collective-permute-start.87 = (f32[4,2,2,64]{3,2,1,0:T(2,128)S(1)}, f32[4,2,2,64]{3,2,1,0:T(2,128)S(1)}, u32[]{:S(2)}, u32[]{:S(2)}) collective-permute-start(f32[4,2,2,64]{3,2,1,0:T(2,128)S(1)} %get-tuple-element.704), channel_id=1, source_target_pairs={{0,4},{4,0},{1,5},{5,1},{2,6},{6,2},{3,7},{7,3},{8,12},{12,8},{9,1... | collective-permute-start | bytes 12296 | tf_op jit(solution)/shard_map/ppermute | solution.py:569
  863.5 20.9 %collective-permute-start.86 = (bf16[64,2048]{1,0:T(8,128)(2,1)S(1)}, bf16[64,2048]{1,0:T(8,128)(2,1)S(1)}, u32[]{:S(2)}, u32[]{:S(2)}) collective-permute-start(bf16[64,2048]{1,0:T(8,128)(2,1)S(1)} %get-tuple-element.703), channel_id=1, source_target_pairs={{0,24},{8,16},{16,8},{24,0},{1,25},{9,17},{17,9},{25,1},{2,26},{10... | collective-permute-start | bytes 786440 | tf_op jit(solution)/shard_map/ppermute | solution.py:569
  865.4 19.7 %collective-permute-start.85 = (bf16[64,2048]{1,0:T(8,128)(2,1)S(1)}, bf16[64,2048]{1,0:T(8,128)(2,1)S(1)}, u32[]{:S(2)}, u32[]{:S(2)}) collective-permute-start(bf16[64,2048]{1,0:T(8,128)(2,1)S(1)} %get-tuple-element.702), channel_id=1, source_target_pairs={{0,8},{8,0},{1,9},{9,1},{2,10},{10,2},{3,11},{11,3},{4,12},{12,4},... | collective-permute-start | bytes 786440 | tf_op jit(solution)/shard_map/ppermute | solution.py:569
  866.5 19.1 %collective-permute-start.84 = (bf16[64,2048]{1,0:T(8,128)(2,1)S(1)}, bf16[64,2048]{1,0:T(8,128)(2,1)S(1)}, u32[]{:S(2)}, u32[]{:S(2)}) collective-permute-start(bf16[64,2048]{1,0:T(8,128)(2,1)S(1)} %get-tuple-element.701), channel_id=1, source_target_pairs={{0,16},{16,0},{1,17},{17,1},{2,18},{18,2},{3,19},{19,3},{4,20},{20... | collective-permute-start | bytes 786440 | tf_op jit(solution)/shard_map/ppermute | solution.py:569
  (125 other events, 1054.5 us)
Sparse Core Ops, SparseCore 0:
  30.8 109.7 all-gather.4
  142.2 218.2 all-gather.6
  530.6 74.5 reduce-scatter.3
  607.6 144.9 reduce-scatter.5
  775.8 93.4 reduce-scatter.7
